TPU v7x, 256 devices: a whole 4x4x8 slice. The times are simulated.
256 devices in a mesh: gz: 16 (over z_hi, x), gy: 16 (over z_lo, y, core).
Axes of the slice: x: 4, y: 4, z: 8 (z_hi: 4, z_lo: 2; z = z_hi * 2 + z_lo), core: 2. Of those that a mesh axis runs over, the one named last changes fastest.
Arguments:
- queries: bfloat16 [32, 64, 16, 256], P('gz', 'gy'), may hold values from -2 to 2
- keys: bfloat16 [32, 64, 16, 256], P('gz', 'gy'), may hold values from -2 to 2
- values: bfloat16 [32, 64, 16, 256], P('gz', 'gy'), may hold values from -6 to 6
- cotangent: bfloat16 [32, 64, 16, 256], P('gz', 'gy'), may hold values from -6 to 6
- conv_weight: bfloat16 [27, 256], replicated, may hold values from -0.625 to 0.625
- block_keep: int32 [16, 16, 2], P('gz', 'gy'), may hold values 0 or 1
Outputs:
- grad_query: bfloat16 [32, 64, 16, 256], P('gz', 'gy')
- grad_key: bfloat16 [32, 64, 16, 256], P('gz', 'gy')
- grad_value: bfloat16 [32, 64, 16, 256], P('gz', 'gy')
- conv_grad: float32 [27, 256], replicated
Inputs may be any that keep to these rules, and one draw needn't show every extreme that they name: `block_keep`: 1 keeps a block, 0 leaves its tokens out as queries and keys.
All inputs are finite; a program needn't handle non-finite values.
Results may differ from a plain program's by a relative error of at most 0.0051.
Values may be sent and summed in bfloat16 or wider, within the bound.
A program may use at most 64 MiB of HBM per device.

v0:
```python
from functools import partial

import jax
import jax.numpy as jnp
import numpy as np
from jax import lax
from jax.sharding import PartitionSpec as P

HEAD = 32
BZ = 2
BY = 4
BX = 8


def extended_2(shard, sides, width):
    for axis, dim in sides:
        devices, length = (lax.axis_size(axis), shard.shape[dim])
        up = [(i, (i + 1) % devices) for i in range(devices - 1)]
        down = [(j, i) for i, j in up]
        last = lax.slice_in_dim(shard, length - width, length, axis=dim)
        leading = lax.slice_in_dim(shard, 0, width, axis=dim)
        before = lax.ppermute(last, axis, up)
        after = lax.ppermute(leading, axis, down)
        shard = jnp.concatenate([before, shard, after], axis=dim)
    return shard


def token_mask(block_keep):
    expanded = jnp.repeat(block_keep, BZ, axis=0)
    expanded = jnp.repeat(expanded, BY, axis=1)
    return jnp.repeat(expanded, BX, axis=2)


def pad_cols(source, width):
    padding_widths = [(0, 0)] * source.ndim
    padding_widths[2] = (width, width)
    return jnp.pad(source, padding_widths)


def tile_index(count, block):
    return np.arange(count // block)[:, None] * block + np.arange(block + 4)[None, :]


def to_tiles(extended, depth, rows_y, lateral_columns, group_x):
    tiled = jnp.take(extended, tile_index(depth, BZ), axis=0)
    tiled = jnp.take(tiled, tile_index(rows_y, BY), axis=2)
    tiled = jnp.take(tiled, tile_index(lateral_columns, group_x), axis=4)
    tiled = jnp.transpose(tiled, (0, 2, 4, 1, 3, 5, 6))
    return tiled.reshape(-1, (BZ + 4) * (BY + 4) * (group_x + 4), extended.shape[-1])


def to_blocks(source, group_x):
    depth, rows_y, lateral_columns, channels = source.shape
    shaped = source.reshape(
        depth // BZ, BZ, rows_y // BY, BY, lateral_columns // group_x, group_x, channels
    )
    shaped = jnp.transpose(shaped, (0, 2, 4, 1, 3, 5, 6))
    return shaped.reshape(-1, BZ * BY * group_x, channels)


def from_blocks(blocks, depth, rows_y, lateral_columns, group_x):
    channels = blocks.shape[-1]
    shaped = blocks.reshape(
        depth // BZ, rows_y // BY, lateral_columns // group_x, BZ, BY, group_x, channels
    )
    shaped = jnp.transpose(shaped, (0, 3, 1, 4, 2, 5, 6))
    return shaped.reshape(depth, rows_y, lateral_columns, channels)


def window_table(group_x):
    own_grid = np.meshgrid(np.arange(BZ), np.arange(BY), np.arange(group_x), indexing="ij")
    brick_lattice = np.meshgrid(
        np.arange(BZ + 4), np.arange(BY + 4), np.arange(group_x + 4), indexing="ij"
    )
    inside = np.ones((BZ * BY * group_x, (BZ + 4) * (BY + 4) * (group_x + 4)), dtype=bool)
    for own_line, tile_line in zip(own_grid, brick_lattice):
        spacing = tile_line.reshape(-1)[None, :] - own_line.reshape(-1)[:, None]
        inside = inside & (spacing >= 0) & (spacing <= 4)
    return jnp.asarray(inside)


def fold_rims(source, dim, count):
    lower = lax.slice_in_dim(source, 0, 2, axis=dim)
    middle = lax.slice_in_dim(source, 4, count + 4, axis=dim)
    upper = lax.slice_in_dim(source, count + 6, count + 8, axis=dim)
    low_widths = [(0, 0)] * source.ndim
    low_widths[dim] = (0, count - 2)
    high_widths = [(0, 0)] * source.ndim
    high_widths[dim] = (count - 2, 0)
    return middle + jnp.pad(lower, low_widths) + jnp.pad(upper, high_widths)


def shards(queries, keys, values, cotangent, conv_weight, block_keep):
    depth, rows_y, lateral_columns, channels = queries.shape
    group_x = min(lateral_columns, 2 * BX)
    head_count = channels // HEAD
    scaling = HEAD ** (-0.5)
    own_mask = token_mask(block_keep).astype(jnp.bfloat16)
    keys_ext, values_ext, gradients_extended, mask_ext = (
        extended_2(keys, (("gz", 0), ("gy", 1)), 2),
        extended_2(values, (("gz", 0), ("gy", 1)), 2),
        extended_2(cotangent, (("gz", 0), ("gy", 1)), 2),
        extended_2(own_mask, (("gz", 0), ("gy", 1)), 2),
    )
    tiler = partial(
        to_tiles, depth=depth, rows_y=rows_y, lateral_columns=lateral_columns, group_x=group_x
    )
    key_tiles = tiler(pad_cols(keys_ext, 2))
    value_tiles = tiler(pad_cols(values_ext, 2))
    mask_tiles = tiler(pad_cols(mask_ext, 2)[..., None])[..., 0].astype(jnp.float32)
    query_blocks = to_blocks(queries, group_x)
    grad_blocks = to_blocks(cotangent, group_x)
    query_mask = to_blocks(own_mask[..., None], group_x)[..., 0].astype(jnp.float32)
    inside = window_table(group_x)
    key_valid = inside[None, :, :] & (mask_tiles > 0.5)[:, None, :]
    ext_zero = jnp.zeros((depth + 4, rows_y + 4, lateral_columns + 4, HEAD), jnp.float32)
    _, fold_tiles = jax.vjp(tiler, ext_zero)
    per_head_lookup_derivative, head_dk, head_dv, total_list, delta_list = ([], [], [], [], [])
    for head_index in range(head_count):
        columns = slice(head_index * HEAD, (head_index + 1) * HEAD)
        query_portion = query_blocks[..., columns]
        matching_share = key_tiles[..., columns]
        payload_share = value_tiles[..., columns]
        gradient_portion = grad_blocks[..., columns]
        scores = (
            jnp.einsum(
                "txv,tjv->txj", query_portion, matching_share, preferred_element_type=jnp.float32
            )
            * scaling
        )
        weights = jnp.where(key_valid, jnp.exp(scores), 0.0)
        totals = jnp.sum(weights, axis=2) + (1.0 - query_mask)
        probs = weights * (query_mask / totals)[:, :, None]
        softmax_lowered_precision = probs.astype(jnp.bfloat16)
        attended = jnp.einsum(
            "wig,wgt->wit",
            softmax_lowered_precision,
            payload_share,
            preferred_element_type=jnp.float32,
        )
        deltas = jnp.sum(gradient_portion.astype(jnp.float32) * attended, axis=2)
        dprobs = jnp.einsum(
            "txv,tjv->txj", gradient_portion, payload_share, preferred_element_type=jnp.float32
        )
        logit_derivatives = (scaling * probs * (dprobs - deltas[:, :, None])).astype(jnp.bfloat16)
        per_head_lookup_derivative.append(
            jnp.einsum(
                "wig,wgt->wit",
                logit_derivatives,
                matching_share,
                preferred_element_type=jnp.float32,
            )
        )
        key_tile_grad = jnp.einsum(
            "jfx,jfe->jxe", logit_derivatives, query_portion, preferred_element_type=jnp.float32
        )
        value_tile_grad = jnp.einsum(
            "jfx,jfe->jxe",
            softmax_lowered_precision,
            gradient_portion,
            preferred_element_type=jnp.float32,
        )
        head_dk.append(fold_tiles(key_tile_grad)[0])
        head_dv.append(fold_tiles(value_tile_grad)[0])
    grad_query = from_blocks(
        jnp.concatenate(per_head_lookup_derivative, axis=2), depth, rows_y, lateral_columns, group_x
    ).astype(jnp.bfloat16)
    key_grad_ext = jnp.concatenate(head_dk, axis=3)[:, :, 2 : lateral_columns + 2]
    value_grad_ext = jnp.concatenate(head_dv, axis=3)[:, :, 2 : lateral_columns + 2]
    key_rims, value_rims = (
        extended_2(key_grad_ext, (("gz", 0), ("gy", 1)), 2),
        extended_2(value_grad_ext, (("gz", 0), ("gy", 1)), 2),
    )
    key_grad_sum = fold_rims(fold_rims(key_rims, 0, depth), 1, rows_y)
    value_grad_sum = fold_rims(fold_rims(value_rims, 0, depth), 1, rows_y)
    grad_near = pad_cols(gradients_extended[1 : depth + 3, 1 : rows_y + 3].astype(jnp.float32), 1)
    value_near = pad_cols(values_ext[1 : depth + 3, 1 : rows_y + 3].astype(jnp.float32), 1)
    grad_local = cotangent.astype(jnp.float32)
    filter_full = conv_weight.astype(jnp.float32)
    conv_values = jnp.zeros(queries.shape, jnp.float32)
    filter_terms = []
    for shift_z in range(3):
        for shift_y in range(3):
            for shift_x in range(3):
                row_index = shift_z * 9 + shift_y * 3 + shift_x
                conv_values = (
                    conv_values
                    + filter_full[row_index]
                    * grad_near[
                        2 - shift_z : 2 - shift_z + depth,
                        2 - shift_y : 2 - shift_y + rows_y,
                        2 - shift_x : 2 - shift_x + lateral_columns,
                    ]
                )
                filter_terms.append(
                    jnp.sum(
                        grad_local
                        * value_near[
                            shift_z : shift_z + depth,
                            shift_y : shift_y + rows_y,
                            shift_x : shift_x + lateral_columns,
                        ],
                        axis=(0, 1, 2),
                    )
                )
    filter_total = lax.psum(jnp.stack(filter_terms), ("gz", "gy"))
    token_count = depth * rows_y * lateral_columns * lax.axis_size("gz") * lax.axis_size("gy")
    conv_grad = filter_total * token_count ** (-0.5)
    grad_key = key_grad_sum.astype(jnp.bfloat16)
    grad_value = (value_grad_sum + conv_values).astype(jnp.bfloat16)
    return (grad_query, grad_key, grad_value, conv_grad)


def solution(mesh):
    in_specs = (
        P("gz", "gy", None, None),
        P("gz", "gy", None, None),
        P("gz", "gy", None, None),
        P("gz", "gy", None, None),
        P(),
        P("gz", "gy", None),
    )
    out_specs = (
        P("gz", "gy", None, None),
        P("gz", "gy", None, None),
        P("gz", "gy", None, None),
        P(),
    )
    return jax.shard_map(shards, mesh=mesh, in_specs=in_specs, out_specs=out_specs, check_vma=False)
```

profile of v0, /device:TPU:7, one launch (start us, length us, event | category | flops | bytes accessed | tf_op | source)
XLA Modules:
  0.0 445.6 jit_solution(906604241794630400)
XLA Ops:
  1.5 4.8 %collective-permute-start = (bf16[2,4,16]{2,1,0:T(4,128)(2,1)S(1)}, bf16[2,4,16]{2,1,0:T(4,128)(2,1)S(1)}, u32[]{:S(2)}, u32[]{:S(2)}) collective-permute-start(bf16[2,4,16]{2,1,0:T(4,128)(2,1)S(1)} %broadcast_in_dim.178), channel_id=1, source_target_pairs={{0,16},{16,32},{32,48},{48,64},{64,80},{80,96},{96,112},{112,128},... | collective-permute-start | bytes 776 | tf_op jit(solution)/shard_map/ppermute | solution.py:22
  8.3 6.4 %collective-permute-start.4 = (bf16[2,4,16,256]{3,2,1,0:T(8,128)(2,1)}, bf16[2,4,16,256]{3,2,1,0:T(8,128)(2,1)S(1)}, u32[]{:S(2)}, u32[]{:S(2)}) collective-permute-start(bf16[2,4,16,256]{3,2,1,0:T(8,128)(2,1)} %param.26), channel_id=1, source_target_pairs={{0,16},{16,32},{32,48},{48,64},{64,80},{80,96},{96,112},{112,128},... | collective-permute-start | bytes 196616 | tf_op jit(solution)/shard_map/ppermute | solution.py:22
  17.5 6.4 %collective-permute-start.20 = (bf16[2,4,16,256]{3,1,2,0:T(4,128)(2,1)S(1)}, bf16[2,4,16,256]{3,1,2,0:T(4,128)(2,1)S(1)}, u32[]{:S(2)}, u32[]{:S(2)}) collective-permute-start(bf16[2,4,16,256]{3,1,2,0:T(4,128)(2,1)S(1)} %copy.262), channel_id=1, source_target_pairs={{0,16},{16,32},{32,48},{48,64},{64,80},{80,96},{96,112},{112,128},... | collective-permute-start | bytes 196616 | tf_op jit(solution)/shard_map/ppermute | solution.py:22
  31.8 5.2 %collective-permute-start.2 = (bf16[6,2,16]{2,1,0:T(2,128)(2,1)S(1)}, bf16[6,2,16]{2,1,0:T(2,128)(2,1)S(1)}, u32[]{:S(2)}, u32[]{:S(2)}) collective-permute-start(bf16[6,2,16]{2,1,0:T(2,128)(2,1)S(1)} %get-tuple-element.95), channel_id=1, source_target_pairs={{0,1},{1,2},{2,3},{3,4},{4,5},{5,6},{6,7},{7,8},{8,9},{9,10},{10,1... | collective-permute-start | bytes 1160 | tf_op jit(solution)/shard_map/ppermute | solution.py:22
  42.9 6.4 %collective-permute-start.8 = (bf16[2,4,16,256]{3,2,1,0:T(8,128)(2,1)S(1)}, bf16[2,4,16,256]{3,2,1,0:T(8,128)(2,1)S(1)}, u32[]{:S(2)}, u32[]{:S(2)}) collective-permute-start(bf16[2,4,16,256]{3,2,1,0:T(8,128)(2,1)S(1)} %copy-done.66), channel_id=1, source_target_pairs={{0,16},{16,32},{32,48},{48,64},{64,80},{80,96},{96,112},{112,128},... | collective-permute-start | bytes 196616 | tf_op jit(solution)/shard_map/ppermute | solution.py:22
  53.6 4.2 collective-permute-start.6
  60.7 3.6 collective-permute-start.22
  67.1 3.6 collective-permute-start.10
  83.7 4.1 scatter_fusion.30
  95.0 3.9 scatter_fusion.33
  103.6 2.7 scatter_fusion.36
  116.9 3.9 scatter_fusion.42
  127.9 4.3 scatter_fusion.45
  156.0 2.9 scatter_fusion.47
  162.0 2.8 scatter_fusion.29
  164.8 3.2 concatenate.57
  178.0 2.9 scatter_fusion.21
  188.3 3.9 scatter_fusion.18
  200.9 3.9 scatter_fusion.15
  213.2 3.9 scatter_fusion.12
  225.8 3.9 scatter_fusion.9
  238.6 3.9 scatter_fusion.6
  251.2 3.9 scatter_fusion.3
  280.2 2.7 scatter_fusion.5
  284.2 3.7 concatenate.54
  297.7 6.8 %collective-permute-start.16 = (f32[2,8,16,256]{3,1,2,0:T(8,128)}, f32[2,8,16,256]{3,1,2,0:T(8,128)S(1)}, u32[]{:S(2)}, u32[]{:S(2)}) collective-permute-start(f32[2,8,16,256]{3,1,2,0:T(8,128)} %get-tuple-element.50), channel_id=1, source_target_pairs={{0,16},{16,32},{32,48},{48,64},{64,80},{80,96},{96,112},{112,128},... | collective-permute-start | bytes 786440 | tf_op jit(solution)/shard_map/ppermute | solution.py:22
  306.4 6.4 %collective-permute-start.12 = (f32[2,8,16,256]{3,1,2,0:T(8,128)}, f32[2,8,16,256]{3,1,2,0:T(8,128)S(1)}, u32[]{:S(2)}, u32[]{:S(2)}) collective-permute-start(f32[2,8,16,256]{3,1,2,0:T(8,128)} %get-tuple-element.52), channel_id=1, source_target_pairs={{0,16},{16,32},{32,48},{48,64},{64,80},{80,96},{96,112},{112,128},... | collective-permute-start | bytes 786440 | tf_op jit(solution)/shard_map/ppermute | solution.py:22
  324.0 89.1 %psum.7 = f32[27,256]{1,0:T(8,128)S(1)} all-reduce(f32[27,256]{1,0:T(8,128)S(1)} %stack.111), channel_id=1, replica_groups=mesh['gz'=16,'gy'=16] {'gz','gy'}, use_global_device_ids=true, to_apply=%region_91.95 | all-reduce | flops 6912 | bytes 55296 | tf_op jit(solution)/shard_map/psum | solution.py:206
  413.1 3.4 collective-permute-start.13
  423.1 8.5 %collective-permute-done.13 = f32[2,8,16,256]{3,1,2,0:T(8,128)S(1)} collective-permute-done((f32[2,8,16,256]{3,1,2,0:T(8,128)}, f32[2,8,16,256]{3,1,2,0:T(8,128)S(1)}, u32[]{:S(2)}, u32[]{:S(2)}) %collective-permute-start.13) | collective-permute-done | bytes 262176 | tf_op jit(solution)/shard_map/ppermute | solution.py:23
  431.8 3.4 collective-permute-start.14
  439.8 4.2 collective-permute-done.15
  (568 shorter events, 218.5 us)
Async XLA Ops:
  1.5 30.3 %collective-permute-start = (bf16[2,4,16]{2,1,0:T(4,128)(2,1)S(1)}, bf16[2,4,16]{2,1,0:T(4,128)(2,1)S(1)}, u32[]{:S(2)}, u32[]{:S(2)}) collective-permute-start(bf16[2,4,16]{2,1,0:T(4,128)(2,1)S(1)} %broadcast_in_dim.178), channel_id=1, source_target_pairs={{0,16},{16,32},{32,48},{48,64},{64,80},{80,96},{96,112},{112,128},... | collective-permute-start | bytes 776 | tf_op jit(solution)/shard_map/ppermute | solution.py:22
  6.3 25.5 %collective-permute-start.1 = (bf16[2,4,16]{2,1,0:T(4,128)(2,1)S(1)}, bf16[2,4,16]{2,1,0:T(4,128)(2,1)S(1)}, u32[]{:S(2)}, u32[]{:S(2)}) collective-permute-start(bf16[2,4,16]{2,1,0:T(4,128)(2,1)S(1)} %broadcast_in_dim.178), channel_id=1, source_target_pairs={{16,0},{32,16},{48,32},{64,48},{80,64},{96,80},{112,96},{128,112},... | collective-permute-start | bytes 776 | tf_op jit(solution)/shard_map/ppermute | solution.py:23
  8.3 43.3 %collective-permute-start.4 = (bf16[2,4,16,256]{3,2,1,0:T(8,128)(2,1)}, bf16[2,4,16,256]{3,2,1,0:T(8,128)(2,1)S(1)}, u32[]{:S(2)}, u32[]{:S(2)}) collective-permute-start(bf16[2,4,16,256]{3,2,1,0:T(8,128)(2,1)} %param.26), channel_id=1, source_target_pairs={{0,16},{16,32},{32,48},{48,64},{64,80},{80,96},{96,112},{112,128},... | collective-permute-start | bytes 196616 | tf_op jit(solution)/shard_map/ppermute | solution.py:22
  14.6 38.9 %collective-permute-start.5 = (bf16[2,4,16,256]{3,2,1,0:T(8,128)(2,1)}, bf16[2,4,16,256]{3,2,1,0:T(8,128)(2,1)S(1)}, u32[]{:S(2)}, u32[]{:S(2)}) collective-permute-start(bf16[2,4,16,256]{3,2,1,0:T(8,128)(2,1)} %param.26), channel_id=1, source_target_pairs={{16,0},{32,16},{48,32},{64,48},{80,64},{96,80},{112,96},{128,112},... | collective-permute-start | bytes 196616 | tf_op jit(solution)/shard_map/ppermute | solution.py:23
  17.5 40.3 %collective-permute-start.20 = (bf16[2,4,16,256]{3,1,2,0:T(4,128)(2,1)S(1)}, bf16[2,4,16,256]{3,1,2,0:T(4,128)(2,1)S(1)}, u32[]{:S(2)}, u32[]{:S(2)}) collective-permute-start(bf16[2,4,16,256]{3,1,2,0:T(4,128)(2,1)S(1)} %copy.262), channel_id=1, source_target_pairs={{0,16},{16,32},{32,48},{48,64},{64,80},{80,96},{96,112},{112,128},... | collective-permute-start | bytes 196616 | tf_op jit(solution)/shard_map/ppermute | solution.py:22
  27.0 134.9 %copy-start.57 = (s32[6]{0:T(128)}, s32[6]{0:T(128)S(1)}, u32[]{:S(2)}) copy-start(s32[6]{0:T(128)S(1)} %iota.3) | copy-start | bytes 76
  27.1 118.4 %copy-start.59 = (s32[8]{0:T(128)}, s32[8]{0:T(128)S(1)}, u32[]{:S(2)}) copy-start(s32[8]{0:T(128)S(1)} %iota.4) | copy-start | bytes 100
  27.1 115.5 %copy-start.61 = (s32[20]{0:T(128)}, s32[20]{0:T(128)S(1)}, u32[]{:S(2)}) copy-start(s32[20]{0:T(128)S(1)} %iota.5) | copy-start | bytes 244
  31.8 9.1 %collective-permute-start.2 = (bf16[6,2,16]{2,1,0:T(2,128)(2,1)S(1)}, bf16[6,2,16]{2,1,0:T(2,128)(2,1)S(1)}, u32[]{:S(2)}, u32[]{:S(2)}) collective-permute-start(bf16[6,2,16]{2,1,0:T(2,128)(2,1)S(1)} %get-tuple-element.95), channel_id=1, source_target_pairs={{0,1},{1,2},{2,3},{3,4},{4,5},{5,6},{6,7},{7,8},{8,9},{9,10},{10,1... | collective-permute-start | bytes 1160 | tf_op jit(solution)/shard_map/ppermute | solution.py:22
  37.0 5.9 %collective-permute-start.3 = (bf16[6,2,16]{2,1,0:T(2,128)(2,1)S(1)}, bf16[6,2,16]{2,1,0:T(2,128)(2,1)S(1)}, u32[]{:S(2)}, u32[]{:S(2)}) collective-permute-start(bf16[6,2,16]{2,1,0:T(2,128)(2,1)S(1)} %get-tuple-element.96), channel_id=1, source_target_pairs={{1,0},{2,1},{3,2},{4,3},{5,4},{6,5},{7,6},{8,7},{9,8},{10,9},{11,1... | collective-permute-start | bytes 1160 | tf_op jit(solution)/shard_map/ppermute | solution.py:23
  41.0 18.8 %collective-permute-start.21 = (bf16[2,4,16,256]{3,1,2,0:T(4,128)(2,1)S(1)}, bf16[2,4,16,256]{3,1,2,0:T(4,128)(2,1)S(1)}, u32[]{:S(2)}, u32[]{:S(2)}) collective-permute-start(bf16[2,4,16,256]{3,1,2,0:T(4,128)(2,1)S(1)} %copy.262), channel_id=1, source_target_pairs={{16,0},{32,16},{48,32},{64,48},{80,64},{96,80},{112,96},{128,112},... | collective-permute-start | bytes 196616 | tf_op jit(solution)/shard_map/ppermute | solution.py:23
  42.9 21.5 %collective-permute-start.8 = (bf16[2,4,16,256]{3,2,1,0:T(8,128)(2,1)S(1)}, bf16[2,4,16,256]{3,2,1,0:T(8,128)(2,1)S(1)}, u32[]{:S(2)}, u32[]{:S(2)}) collective-permute-start(bf16[2,4,16,256]{3,2,1,0:T(8,128)(2,1)S(1)} %copy-done.66), channel_id=1, source_target_pairs={{0,16},{16,32},{32,48},{48,64},{64,80},{80,96},{96,112},{112,128},... | collective-permute-start | bytes 196616 | tf_op jit(solution)/shard_map/ppermute | solution.py:22
  51.6 14.8 %collective-permute-start.9 = (bf16[2,4,16,256]{3,2,1,0:T(8,128)(2,1)S(1)}, bf16[2,4,16,256]{3,2,1,0:T(8,128)(2,1)S(1)}, u32[]{:S(2)}, u32[]{:S(2)}) collective-permute-start(bf16[2,4,16,256]{3,2,1,0:T(8,128)(2,1)S(1)} %copy-done.66), channel_id=1, source_target_pairs={{16,0},{32,16},{48,32},{64,48},{80,64},{96,80},{112,96},{128,112},... | collective-permute-start | bytes 196616 | tf_op jit(solution)/shard_map/ppermute | solution.py:23
  53.6 17.2 %collective-permute-start.6 = (bf16[6,2,16,256]{3,2,1,0:T(8,128)(2,1)S(1)}, bf16[6,2,16,256]{3,2,1,0:T(8,128)(2,1)S(1)}, u32[]{:S(2)}, u32[]{:S(2)}) collective-permute-start(bf16[6,2,16,256]{3,2,1,0:T(8,128)(2,1)S(1)} %get-tuple-element.58), channel_id=1, source_target_pairs={{0,1},{1,2},{2,3},{3,4},{4,5},{5,6},{6,7},{7,8},{8,9},{9,10},{10,1... | collective-permute-start | bytes 294920 | tf_op jit(solution)/shard_map/ppermute | solution.py:22
  57.8 14.9 %collective-permute-start.7 = (bf16[6,2,16,256]{3,2,1,0:T(8,128)(2,1)S(1)}, bf16[6,2,16,256]{3,2,1,0:T(8,128)(2,1)S(1)}, u32[]{:S(2)}, u32[]{:S(2)}) collective-permute-start(bf16[6,2,16,256]{3,2,1,0:T(8,128)(2,1)S(1)} %get-tuple-element.59), channel_id=1, source_target_pairs={{1,0},{2,1},{3,2},{4,3},{5,4},{6,5},{7,6},{8,7},{9,8},{10,9},{11,1... | collective-permute-start | bytes 294920 | tf_op jit(solution)/shard_map/ppermute | solution.py:23
  60.7 352.3 %collective-permute-start.22 = (bf16[6,2,16,256]{3,1,2,0:T(2,128)(2,1)}, bf16[6,2,16,256]{3,1,2,0:T(2,128)(2,1)}, u32[]{:S(2)}, u32[]{:S(2)}) collective-permute-start(bf16[6,2,16,256]{3,1,2,0:T(2,128)(2,1)} %get-tuple-element.54), channel_id=1, source_target_pairs={{0,1},{1,2},{2,3},{3,4},{4,5},{5,6},{6,7},{7,8},{8,9},{9,10},{10,1... | collective-permute-start | bytes 294920 | tf_op jit(solution)/shard_map/ppermute | solution.py:22
  64.4 352.1 %collective-permute-start.23 = (bf16[6,2,16,256]{3,1,2,0:T(2,128)(2,1)}, bf16[6,2,16,256]{3,1,2,0:T(2,128)(2,1)}, u32[]{:S(2)}, u32[]{:S(2)}) collective-permute-start(bf16[6,2,16,256]{3,1,2,0:T(2,128)(2,1)} %get-tuple-element.55), channel_id=1, source_target_pairs={{1,0},{2,1},{3,2},{4,3},{5,4},{6,5},{7,6},{8,7},{9,8},{10,9},{11,1... | collective-permute-start | bytes 294920 | tf_op jit(solution)/shard_map/ppermute | solution.py:23
  67.1 101.9 %collective-permute-start.10 = (bf16[6,2,16,256]{3,2,1,0:T(8,128)(2,1)}, bf16[6,2,16,256]{3,2,1,0:T(8,128)(2,1)}, u32[]{:S(2)}, u32[]{:S(2)}) collective-permute-start(bf16[6,2,16,256]{3,2,1,0:T(8,128)(2,1)} %get-tuple-element.56), channel_id=1, source_target_pairs={{0,1},{1,2},{2,3},{3,4},{4,5},{5,6},{6,7},{7,8},{8,9},{9,10},{10,1... | collective-permute-start | bytes 294920 | tf_op jit(solution)/shard_map/ppermute | solution.py:22
  70.8 98.2 %collective-permute-start.11 = (bf16[6,2,16,256]{3,2,1,0:T(8,128)(2,1)}, bf16[6,2,16,256]{3,2,1,0:T(8,128)(2,1)}, u32[]{:S(2)}, u32[]{:S(2)}) collective-permute-start(bf16[6,2,16,256]{3,2,1,0:T(8,128)(2,1)} %get-tuple-element.57), channel_id=1, source_target_pairs={{1,0},{2,1},{3,2},{4,3},{5,4},{6,5},{7,6},{8,7},{9,8},{10,9},{11,1... | collective-permute-start | bytes 294920 | tf_op jit(solution)/shard_map/ppermute | solution.py:23
  80.1 56.2 %copy-start.12 = (f32[128,960]{0,1:T(8,128)}, f32[128,960]{0,1:T(8,128)S(1)}, u32[]{:S(2)}) copy-start(f32[128,960]{0,1:T(8,128)S(1)} %get-tuple-element.120) | copy-start | bytes 1474564
  80.5 55.9 %copy-start.10 = (f32[128,960]{0,1:T(8,128)}, f32[128,960]{0,1:T(8,128)S(1)}, u32[]{:S(2)}) copy-start(f32[128,960]{0,1:T(8,128)S(1)} %get-tuple-element.122) | copy-start | bytes 1474564
  80.5 55.8 %copy-start.75 = (f32[128]{0:T(128)}, f32[128]{0:T(128)S(1)}, u32[]{:S(2)}) copy-start(f32[128]{0:T(128)S(1)} %get-tuple-element.104) | copy-start | bytes 1540
  80.6 55.8 %copy-start.77 = (f32[128]{0:T(128)}, f32[128]{0:T(128)S(1)}, u32[]{:S(2)}) copy-start(f32[128]{0:T(128)S(1)} %get-tuple-element.103) | copy-start | bytes 1540
  297.7 119.9 %collective-permute-start.16 = (f32[2,8,16,256]{3,1,2,0:T(8,128)}, f32[2,8,16,256]{3,1,2,0:T(8,128)S(1)}, u32[]{:S(2)}, u32[]{:S(2)}) collective-permute-start(f32[2,8,16,256]{3,1,2,0:T(8,128)} %get-tuple-element.50), channel_id=1, source_target_pairs={{0,16},{16,32},{32,48},{48,64},{64,80},{80,96},{96,112},{112,128},... | collective-permute-start | bytes 786440 | tf_op jit(solution)/shard_map/ppermute | solution.py:22
  304.5 113.1 %collective-permute-start.17 = (f32[2,8,16,256]{3,1,2,0:T(8,128)}, f32[2,8,16,256]{3,1,2,0:T(8,128)S(1)}, u32[]{:S(2)}, u32[]{:S(2)}) collective-permute-start(f32[2,8,16,256]{3,1,2,0:T(8,128)} %get-tuple-element.51), channel_id=1, source_target_pairs={{16,0},{32,16},{48,32},{64,48},{80,64},{96,80},{112,96},{128,112},... | collective-permute-start | bytes 786440 | tf_op jit(solution)/shard_map/ppermute | solution.py:23
  306.4 116.6 %collective-permute-start.12 = (f32[2,8,16,256]{3,1,2,0:T(8,128)}, f32[2,8,16,256]{3,1,2,0:T(8,128)S(1)}, u32[]{:S(2)}, u32[]{:S(2)}) collective-permute-start(f32[2,8,16,256]{3,1,2,0:T(8,128)} %get-tuple-element.52), channel_id=1, source_target_pairs={{0,16},{16,32},{32,48},{48,64},{64,80},{80,96},{96,112},{112,128},... | collective-permute-start | bytes 786440 | tf_op jit(solution)/shard_map/ppermute | solution.py:22
  322.2 94.4 %copy-start.46 = (bf16[6,4,16,256]{3,1,2,0:T(4,128)(2,1)S(1)}, bf16[6,4,16,256]{3,1,2,0:T(4,128)(2,1)}, u32[]{:S(2)}) copy-start(bf16[6,4,16,256]{3,1,2,0:T(4,128)(2,1)} %copy-done.45) | copy-start | bytes 589828
  413.1 18.5 %collective-permute-start.13 = (f32[2,8,16,256]{3,1,2,0:T(8,128)}, f32[2,8,16,256]{3,1,2,0:T(8,128)S(1)}, u32[]{:S(2)}, u32[]{:S(2)}) collective-permute-start(f32[2,8,16,256]{3,1,2,0:T(8,128)} %get-tuple-element.53), channel_id=1, source_target_pairs={{16,0},{32,16},{48,32},{64,48},{80,64},{96,80},{112,96},{128,112},... | collective-permute-start | bytes 786440 | tf_op jit(solution)/shard_map/ppermute | solution.py:23
  417.9 19.6 %collective-permute-start.18 = (f32[10,2,16,256]{3,1,2,0:T(2,128)S(1)}, f32[10,2,16,256]{3,1,2,0:T(2,128)S(1)}, u32[]{:S(2)}, u32[]{:S(2)}) collective-permute-start(f32[10,2,16,256]{3,1,2,0:T(2,128)S(1)} %get-tuple-element.46), channel_id=1, source_target_pairs={{0,1},{1,2},{2,3},{3,4},{4,5},{5,6},{6,7},{7,8},{8,9},{9,10},{10,1... | collective-permute-start | bytes 983048 | tf_op jit(solution)/shard_map/ppermute | solution.py:22
  420.5 17.0 %collective-permute-start.19 = (f32[10,2,16,256]{3,1,2,0:T(2,128)S(1)}, f32[10,2,16,256]{3,1,2,0:T(2,128)S(1)}, u32[]{:S(2)}, u32[]{:S(2)}) collective-permute-start(f32[10,2,16,256]{3,1,2,0:T(2,128)S(1)} %get-tuple-element.47), channel_id=1, source_target_pairs={{1,0},{2,1},{3,2},{4,3},{5,4},{6,5},{7,6},{8,7},{9,8},{10,9},{11,1... | collective-permute-start | bytes 983048 | tf_op jit(solution)/shard_map/ppermute | solution.py:23
  431.8 7.9 %collective-permute-start.14 = (f32[10,2,16,256]{3,1,2,0:T(2,128)S(1)}, f32[10,2,16,256]{3,1,2,0:T(2,128)S(1)}, u32[]{:S(2)}, u32[]{:S(2)}) collective-permute-start(f32[10,2,16,256]{3,1,2,0:T(2,128)S(1)} %get-tuple-element.48), channel_id=1, source_target_pairs={{0,1},{1,2},{2,3},{3,4},{4,5},{5,6},{6,7},{7,8},{8,9},{9,10},{10,1... | collective-permute-start | bytes 983048 | tf_op jit(solution)/shard_map/ppermute | solution.py:22
  435.6 8.4 %collective-permute-start.15 = (f32[10,2,16,256]{3,1,2,0:T(2,128)S(1)}, f32[10,2,16,256]{3,1,2,0:T(2,128)S(1)}, u32[]{:S(2)}, u32[]{:S(2)}) collective-permute-start(f32[10,2,16,256]{3,1,2,0:T(2,128)S(1)} %get-tuple-element.49), channel_id=1, source_target_pairs={{1,0},{2,1},{3,2},{4,3},{5,4},{6,5},{7,6},{8,7},{9,8},{10,9},{11,1... | collective-permute-start | bytes 983048 | tf_op jit(solution)/shard_map/ppermute | solution.py:23
  (115 other events, 666.6 us)
where the time goes:
time: 454 us; the launch traced here: 446 us
  other arithmetic  124 us (27%)
  local copies, waits for them, and re-layouts  98.4 us (22%)
  blocking collectives  89.1 us (20%)
  starting transfers between devices  84.2 us (19%)
  matrix products  33.1 us (7%)
  waiting for transfers between devices  12.8 us (3%)
    psum x1, blocking collectives, shards(): filter_total = lax.psum(jnp.stack(filter_terms), ('gz', 'gy'))  89.1 us
    ppermute x12, starting transfers between devices, extended_2(): before = lax.ppermute(last, axis, up)  59.7 us
    scatter-add x16, other arithmetic, to_tiles(): tiled = jnp.take(tiled, tile_index(lateral_columns, group_x), axis=4)  56.1 us
    scatter-add x16, other arithmetic, to_tiles(): tiled = jnp.take(tiled, tile_index(rows_y, BY), axis=2)  31.3 us
    scatter-add x16, other arithmetic, to_tiles(): tiled = jnp.take(extended, tile_index(depth, BZ), axis=0)  29.6 us
    ppermute x12, starting transfers between devices, extended_2(): after = lax.ppermute(leading, axis, down)  24.5 us
    unnamed x263, local copies, waits for them, and re-layouts  19.7 us
    ppermute x12, waiting for transfers between devices, extended_2(): after = lax.ppermute(leading, axis, down)  12.7 us
  transfers between devices with their start and end apart: 24, of which 2 were waited for; matrix products, arithmetic and copies ran while one was open for 54% of the time, Pallas kernels for 0%

commit v1 on v0

v1 whole, which is shorter than its diff:
```python
from functools import partial

import jax
import jax.numpy as jnp
from jax import lax
from jax.experimental import pallas as pl
from jax.experimental.pallas import tpu as pltpu
from jax.sharding import PartitionSpec as P

HEAD = 32
BX = 8
LANES = 128
GROUP_HEADS = LANES // HEAD
DEAD = 4.0
LOG2E = 1.4426950408889634
MESH = pl.DeviceIdType.MESH
F32 = jnp.float32
BF16 = jnp.bfloat16


def rounds_of(sections, rows):
    first = [("gy", rows // 2, 2), ("gy", 1, 2)]
    between = [[("gy", 2, rows // 4)]] if rows > 4 else []
    along = []
    stride = 1
    while stride < sections:
        along.append([("gz", stride, min(4, sections // stride))])
        stride *= 4
    return [first] + between + along


def kernel(
    sections,
    rows_n,
    depth,
    rows,
    cols,
    q_ref,
    k_ref,
    v_ref,
    g_ref,
    w_ref,
    keep_ref,
    gq_ref,
    gk_ref,
    gv_ref,
    cg_ref,
    ext,
    acc,
    qm,
    gm,
    shifted,
    filt,
    eights,
    mask,
    part_y,
    got_y,
    part_z,
    got_z,
    terms,
    halo_send,
    halo_recv,
    py_send,
    py_recv,
    pz_send,
    pz_recv,
    sum_send,
    sum_recv,
):
    groups = ext.shape[0]
    tokens = depth * rows * cols
    place = {"gz": lax.axis_index("gz"), "gy": lax.axis_index("gy")}
    gz, gy = place["gz"], place["gy"]
    has = {
        "zm": gz > 0,
        "zp": gz < sections - 1,
        "ym": gy > 0,
        "yp": gy < rows_n - 1,
    }
    device = {"zm": (gz - 1, gy), "zp": (gz + 1, gy), "ym": (gz, gy - 1), "yp": (gz, gy + 1)}
    sum_rounds = rounds_of(sections, rows_n)

    def digit(spec):
        axis, stride, count = spec
        return (place[axis] // stride) % count

    def member_of(digits):
        m = 0
        for spec in digits:
            m = m * spec[2] + digit(spec)
        return m

    def peer(digits, m):
        out = dict(place)
        for spec in reversed(digits):
            axis, stride, count = spec
            want = m % count
            m = m // count
            out[axis] = out[axis] + (want - digit(spec)) * stride
        return (out["gz"], out["gy"])

    def size_of(digits):
        n = 1
        for spec in digits:
            n *= spec[2]
        return n

    barrier = pltpu.get_barrier_semaphore()
    expected = 0
    for side in ("zm", "zp", "ym", "yp"):

        @pl.when(has[side])
        def _(side=side):
            pl.semaphore_signal(barrier, inc=1, device_id=device[side], device_id_type=MESH)

        expected = expected + has[side].astype(jnp.int32)
    for digits in sum_rounds:
        n = size_of(digits)
        me = member_of(digits)
        for step in range(1, n):
            pl.semaphore_signal(
                barrier, inc=1, device_id=peer(digits, (me + step) % n), device_id_type=MESH
            )
        expected = expected + (n - 1)

    keep_low = keep_ref[0, 0, 0].astype(F32)
    keep_high = keep_ref[0, 0, 1].astype(F32)
    row_x = lax.broadcasted_iota(jnp.int32, (cols, LANES), 0)
    row_keep = jnp.where(row_x < BX, keep_low, keep_high)
    lane = lax.broadcasted_iota(jnp.int32, (1, LANES), 1)
    lane_x = lane % cols
    lane_keep = jnp.where(lane_x < BX, keep_low, keep_high)
    lane_head = lane // HEAD

    for g in range(groups):
        part = slice(g * LANES, (g + 1) * LANES)
        own = k_ref[:, :, :, part].astype(F32)
        ext[g, 0, 2 : 2 + depth, 2 : 2 + rows] = jnp.where(row_keep > 0.5, own, DEAD).astype(BF16)
        ext[g, 1, 2 : 2 + depth, 2 : 2 + rows] = v_ref[:, :, :, part]

    pl.semaphore_wait(barrier, expected)

    inner = pl.ds(2, rows)
    low = pl.ds(2, 2)
    high = pl.ds(rows, 2)
    z_own, z_first, z_last = pl.ds(2, depth), pl.ds(0, 2), pl.ds(2 + depth, 2)
    y_first, y_last = pl.ds(0, 2), pl.ds(2 + rows, 2)

    halo = [
        (("zp",), (z_own, inner), (z_first, inner), ("zm",)),
        (("zm",), (z_own, inner), (z_last, inner), ("zp",)),
        (("yp",), (z_own, high), (z_own, y_first), ("ym",)),
        (("ym",), (z_own, low), (z_own, y_last), ("yp",)),
        (("yp", "zm"), (z_first, high), (z_first, y_first), ("ym", "zm")),
        (("ym", "zm"), (z_first, low), (z_first, y_last), ("yp", "zm")),
        (("yp", "zp"), (z_last, high), (z_last, y_first), ("ym", "zp")),
        (("ym", "zp"), (z_last, low), (z_last, y_last), ("yp", "zp")),
    ]

    def both(names):
        found = has[names[0]]
        for name in names[1:]:
            found = jnp.logical_and(found, has[name])
        return found

    def halo_copy(g, slot):
        to, (sz, sy), (dz, dy), _ = halo[slot]
        return pltpu.make_async_remote_copy(
            src_ref=ext.at[g, :, sz, sy],
            dst_ref=ext.at[g, :, dz, dy],
            send_sem=halo_send.at[g, slot],
            recv_sem=halo_recv.at[g, slot],
            device_id=device[to[0]],
            device_id_type=MESH,
        )

    def halo_start(g, slot):
        @pl.when(both(halo[slot][0]))
        def _():
            halo_copy(g, slot).start()

    def halo_sent(g, slot):
        @pl.when(both(halo[slot][0]))
        def _():
            halo_copy(g, slot).wait_send()

    def halo_got(g, slot):
        @pl.when(both(halo[slot][3]))
        def _():
            halo_copy(g, slot).wait_recv()

    for g in range(groups):
        for slot in range(4):
            halo_start(g, slot)

    for side, where in (
        ("zm", (z_first, slice(None))),
        ("zp", (z_last, slice(None))),
        ("ym", (slice(None), y_first)),
        ("yp", (slice(None), y_last)),
    ):

        @pl.when(jnp.logical_not(has[side]))
        def _(side=side, where=where):
            shape = ext[(slice(None), 0) + where].shape
            ext[(slice(None), 0) + where] = jnp.full(shape, DEAD, BF16)
            ext[(slice(None), 1) + where] = jnp.zeros(shape, BF16)
            got = got_z if side[0] == "z" else got_y
            slot = 0 if side[1] == "m" else 1
            got[:, slot] = jnp.zeros(got[:, slot].shape, BF16)

    for o in range(27):
        filt[o] = jnp.broadcast_to(w_ref[o : o + 1].astype(F32), filt.shape[1:])

    def own_row(y, carry):
        for g in range(groups):
            part = slice(g * LANES, (g + 1) * LANES)
            for z in range(depth):
                q_row = q_ref[z, y, :, part].astype(F32)
                g_row = g_ref[z, y, :, part].astype(F32)
                for h in range(GROUP_HEADS):
                    at = pl.ds((z * GROUP_HEADS + h) * cols, cols)
                    mine = lane_head == h
                    qm[g, y, at] = jnp.where(mine, q_row, 0.0).astype(BF16)
                    gm[g, y, at] = jnp.where(mine, g_row, 0.0).astype(BF16)
                none = jnp.zeros((1, LANES), F32)
                shifted[g, 0, z, y] = jnp.concatenate([g_row[1:], none], axis=0)
                shifted[g, 1, z, y] = g_row
                shifted[g, 2, z, y] = jnp.concatenate([none, g_row[:-1]], axis=0)
        return carry

    lax.fori_loop(0, rows, own_row, 0)
    acc[...] = jnp.zeros(acc.shape, F32)
    eights[27:] = jnp.zeros((5, 8, eights.shape[2]), F32)

    octets = (depth * rows * cols // 8, 8, LANES)
    whole = (depth, rows, cols, LANES)

    def filter_values(i, carry):
        oz, oy = i // 3, i % 3
        for g in range(groups):
            part = slice(g * LANES, (g + 1) * LANES)
            total = acc[g, 1, pl.ds(1 + oz, depth), pl.ds(1 + oy, rows)].reshape(octets)
            for ox in range(3):
                total = total + filt[3 * i + ox, :, part] * shifted[g, ox].reshape(octets)
            acc[g, 1, pl.ds(1 + oz, depth), pl.ds(1 + oy, rows)] = total.reshape(whole)
        return carry

    lax.fori_loop(0, 9, filter_values, 0)

    band = jnp.abs(row_x - lane_x) <= 2
    half = lax.broadcasted_iota(jnp.int32, (cols, LANES), 1) // (GROUP_HEADS * cols)

    def make_mask():
        for z in range(depth + 4):
            reach = band
            for own in range(depth):
                if not own <= z <= own + 4:
                    reach = jnp.logical_and(reach, half != own)
            live = jnp.where(reach, 1.0, 0.0)
            mask[z] = jnp.where(ext[0, 0, z].astype(F32) < 3.0, live, 0.0)

    scaling = HEAD**-0.5
    keys_n = (depth + 4) * 5 * cols
    head_row = lax.broadcasted_iota(jnp.int32, (depth * GROUP_HEADS * cols, LANES), 0)
    head_row = (head_row // cols) % GROUP_HEADS
    own_head = head_row == lax.broadcasted_iota(jnp.int32, head_row.shape, 1) // HEAD

    def attend(g):
        part = slice(g * LANES, (g + 1) * LANES)

        def row(y, carry):
            near = pl.ds(y, 5)
            keys = ext[g, 0, :, near].reshape(keys_n, LANES)
            values = ext[g, 1, :, near].reshape(keys_n, LANES)
            queries, grads = qm[g, y], gm[g, y]
            nt = (((1,), (1,)), ((), ()))
            tn = (((0,), (0,)), ((), ()))
            scores = lax.dot_general(keys, queries, nt, preferred_element_type=F32)
            weights = jnp.exp2(scores * (scaling * LOG2E)) * mask[:, near].reshape(keys_n, LANES)
            totals = jnp.sum(weights, axis=0, keepdims=True) + (1.0 - lane_keep)
            probs = weights * (lane_keep / totals)
            probs_low = probs.astype(BF16)
            dprobs = lax.dot_general(values, grads, nt, preferred_element_type=F32)
            deltas = jnp.sum(probs_low.astype(F32) * dprobs, axis=0, keepdims=True)
            dscores = (scaling * probs * (dprobs - deltas)).astype(BF16)
            shape = (depth + 4, 5, cols, LANES)
            acc[g, 1, :, near] += jnp.dot(
                probs_low, grads, preferred_element_type=F32
            ).reshape(shape)
            acc[g, 0, :, near] += jnp.dot(
                dscores, queries, preferred_element_type=F32
            ).reshape(shape)
            dq = lax.dot_general(dscores, keys, tn, preferred_element_type=F32)
            dq = jnp.where(own_head, dq, 0.0).reshape(depth, GROUP_HEADS, cols, LANES)
            gq_ref[:, pl.ds(y, 1), :, part] = jnp.sum(dq, axis=1)[:, None].astype(BF16)
            return carry

        return row

    def part_copy(g, stage, slot):
        if stage == "y":
            src, dst, sends, recvs = part_y, got_y, py_send, py_recv
        else:
            src, dst, sends, recvs = part_z, got_z, pz_send, pz_recv
        to = stage + ("p" if slot == 0 else "m")
        return to, stage + ("m" if slot == 0 else "p"), pltpu.make_async_remote_copy(
            src_ref=src.at[g, slot],
            dst_ref=dst.at[g, slot],
            send_sem=sends.at[g, slot],
            recv_sem=recvs.at[g, slot],
            device_id=device[to],
            device_id_type=MESH,
        )

    def part_start(g, stage):
        for slot in range(2):
            to, _, copy = part_copy(g, stage, slot)

            @pl.when(has[to])
            def _(copy=copy):
                copy.start()

    def part_got(g, stage):
        for slot in range(2):
            _, source, copy = part_copy(g, stage, slot)

            @pl.when(has[source])
            def _(copy=copy):
                copy.wait_recv()

    def part_sent(g, stage):
        for slot in range(2):
            to, _, copy = part_copy(g, stage, slot)

            @pl.when(has[to])
            def _(copy=copy):
                copy.wait_send()

    def send_rows(g):
        part_y[g, 0] = acc[g, :, :, 2 + rows : 4 + rows].astype(BF16)
        part_y[g, 1] = acc[g, :, :, 0:2].astype(BF16)
        part_start(g, "y")

    def send_sections(g):
        part_got(g, "y")
        acc[g, :, :, 2:4] += got_y[g, 0].astype(F32)
        acc[g, :, :, rows : rows + 2] += got_y[g, 1].astype(F32)
        part_z[g, 0] = acc[g, :, 2 + depth : 4 + depth, 2 : 2 + rows].astype(BF16)
        part_z[g, 1] = acc[g, :, 0:2, 2 : 2 + rows].astype(BF16)
        part_start(g, "z")

    def finish(g):
        part = slice(g * LANES, (g + 1) * LANES)
        part_got(g, "z")
        for kind, out in ((0, gk_ref), (1, gv_ref)):
            total = acc[g, kind, 2 : 2 + depth, 2 : 2 + rows]
            total = total + got_z[g, 0, kind].astype(F32) + got_z[g, 1, kind].astype(F32)
            out[:, :, :, part] = total.astype(BF16)

    def filter_terms(g):
        part = slice(g * LANES, (g + 1) * LANES)

        def one(i, carry):
            oz, oy = i // 3, i % 3
            near = ext[g, 1, pl.ds(1 + oz, depth), pl.ds(1 + oy, rows)].astype(F32)
            for ox in range(3):
                product = (near * shifted[g, ox]).reshape(octets)
                eights[3 * i + ox, :, part] = jnp.sum(product, axis=0)
            return carry

        lax.fori_loop(0, 9, one, 0)

    def sum_copy(r, m, step):
        n = size_of(sum_rounds[r])
        return pltpu.make_async_remote_copy(
            src_ref=terms.at[r, m],
            dst_ref=terms.at[r, m],
            send_sem=sum_send.at[r, step],
            recv_sem=sum_recv.at[r, m],
            device_id=peer(sum_rounds[r], (member_of(sum_rounds[r]) + step) % n),
            device_id_type=MESH,
        )

    def sum_begin():
        me = member_of(sum_rounds[0])
        terms[0, me] = jnp.sum(eights[...], axis=1)
        sum_start(0)

    def sum_start(r):
        me = member_of(sum_rounds[r])
        for step in range(1, size_of(sum_rounds[r])):
            sum_copy(r, me, step).start()

    def sum_got(r):
        n = size_of(sum_rounds[r])
        me = member_of(sum_rounds[r])
        for step in range(1, n):
            sum_copy(r, (me + step) % n, step).wait_recv()
        total = terms[r, 0]
        for m in range(1, n):
            total = total + terms[r, m]
        if r + 1 < len(sum_rounds):
            terms[r + 1, member_of(sum_rounds[r + 1])] = total
            sum_start(r + 1)
        else:
            cg_ref[...] = total[0:27] * ((tokens * sections * rows_n) ** -0.5)

    def relay(g):
        halo_got(g, 0)
        halo_start(g, 4)
        halo_start(g, 5)
        halo_got(g, 1)
        halo_start(g, 6)
        halo_start(g, 7)

    def arrived(g):
        for slot in (2, 3, 4, 5, 6, 7):
            halo_got(g, slot)

    relay(0)
    arrived(0)
    make_mask()
    lax.fori_loop(0, rows // 2, attend(0), 0)
    relay(1)
    lax.fori_loop(rows // 2, rows, attend(0), 0)
    send_rows(0)
    filter_terms(0)
    arrived(1)
    filter_terms(1)
    sum_begin()
    lax.fori_loop(0, rows // 2, attend(1), 0)
    send_sections(0)
    sum_got(0)
    lax.fori_loop(rows // 2, rows, attend(1), 0)
    send_rows(1)
    sum_got(1)
    finish(0)
    send_sections(1)
    for r in range(2, len(sum_rounds)):
        sum_got(r)
    finish(1)
    for g in range(groups):
        for slot in range(8):
            halo_sent(g, slot)
        part_sent(g, "y")
        part_sent(g, "z")
    for r in range(len(sum_rounds)):
        for step in range(1, size_of(sum_rounds[r])):
            sum_copy(r, member_of(sum_rounds[r]), step).wait_send()


def shards(sections, rows_n, queries, keys, values, cotangent, conv_weight, block_keep):
    depth, rows, cols, channels = queries.shape
    groups = channels // LANES
    heads_rows = depth * GROUP_HEADS * cols
    sum_rounds = len(rounds_of(sections, rows_n))
    big = jax.ShapeDtypeStruct(queries.shape, BF16)
    vmem = pl.BlockSpec(memory_space=pltpu.VMEM)
    dma = pltpu.SemaphoreType.DMA
    return pl.pallas_call(
        partial(kernel, sections, rows_n, depth, rows, cols),
        out_shape=(big, big, big, jax.ShapeDtypeStruct(conv_weight.shape, F32)),
        in_specs=[vmem] * 5 + [pl.BlockSpec(memory_space=pltpu.SMEM)],
        out_specs=(vmem,) * 4,
        scratch_shapes=[
            pltpu.VMEM((groups, 2, depth + 4, rows + 4, cols, LANES), BF16),
            pltpu.VMEM((groups, 2, depth + 4, rows + 4, cols, LANES), F32),
            pltpu.VMEM((groups, rows, heads_rows, LANES), BF16),
            pltpu.VMEM((groups, rows, heads_rows, LANES), BF16),
            pltpu.VMEM((groups, 3, depth, rows, cols, LANES), F32),
            pltpu.VMEM((27, 8, channels), F32),
            pltpu.VMEM((32, 8, channels), F32),
            pltpu.VMEM((depth + 4, rows + 4, cols, LANES), F32),
            pltpu.VMEM((groups, 2, 2, depth + 4, 2, cols, LANES), BF16),
            pltpu.VMEM((groups, 2, 2, depth + 4, 2, cols, LANES), BF16),
            pltpu.VMEM((groups, 2, 2, 2, rows, cols, LANES), BF16),
            pltpu.VMEM((groups, 2, 2, 2, rows, cols, LANES), BF16),
            pltpu.VMEM((sum_rounds, 4, 32, channels), F32),
            dma((groups, 8)),
            dma((groups, 8)),
            dma((groups, 2)),
            dma((groups, 2)),
            dma((groups, 2)),
            dma((groups, 2)),
            dma((sum_rounds, 4)),
            dma((sum_rounds, 4)),
        ],
        compiler_params=pltpu.CompilerParams(
            collective_id=0, has_side_effects=True, vmem_limit_bytes=32 * 1024 * 1024
        ),
    )(queries, keys, values, cotangent, conv_weight, block_keep)


def solution(mesh):
    in_specs = (
        P("gz", "gy", None, None),
        P("gz", "gy", None, None),
        P("gz", "gy", None, None),
        P("gz", "gy", None, None),
        P(),
        P("gz", "gy", None),
    )
    out_specs = (
        P("gz", "gy", None, None),
        P("gz", "gy", None, None),
        P("gz", "gy", None, None),
        P(),
    )
    return jax.shard_map(
        partial(shards, mesh.shape["gz"], mesh.shape["gy"]),
        mesh=mesh,
        in_specs=in_specs,
        out_specs=out_specs,
        check_vma=False,
    )
```

time: 454 us -> 51.2 us (0.11)
  the two profiles are of different devices: /device:TPU:7 before, /device:TPU:4 now
where the time goes in v1:
time: 51.2 us; the launch traced here: 50.9 us
  Pallas kernels  43 us (84%)
  local copies, waits for them, and re-layouts  7.23 us (14%)
  between operations  0.66 us (1%)
    pallas_call x1, Pallas kernels, shards(): pl.pallas_call(partial(kernel, sections, rows_n, depth, rows, cols), out_...  43 us
    unnamed x16, local copies, waits for them, and re-layouts  7.23 us

profile of v1, /device:TPU:4, one launch (start us, length us, event | category | flops | bytes accessed | tf_op | source)
XLA Modules:
  0.0 50.9 jit_solution(17744855284027570972)
XLA Ops:
  0.6 0.0 copy-start
  0.6 0.8 %copy-done = bf16[2,4,16,256]{3,2,1,0:T(8,128)(2,1)S(1)} copy-done((bf16[2,4,16,256]{3,2,1,0:T(8,128)(2,1)S(1)}, bf16[2,4,16,256]{3,2,1,0:T(8,128)(2,1)}, u32[]{:S(2)}) %copy-start) | copy-done | bytes 65560
  1.5 0.0 copy-start.1
  1.5 0.8 %copy-done.1 = bf16[2,4,16,256]{3,2,1,0:T(8,128)(2,1)S(1)} copy-done((bf16[2,4,16,256]{3,2,1,0:T(8,128)(2,1)S(1)}, bf16[2,4,16,256]{3,2,1,0:T(8,128)(2,1)}, u32[]{:S(2)}) %copy-start.1) | copy-done | bytes 65560
  2.3 0.0 copy-start.2
  2.3 0.8 %copy-done.2 = bf16[2,4,16,256]{3,2,1,0:T(8,128)(2,1)S(1)} copy-done((bf16[2,4,16,256]{3,2,1,0:T(8,128)(2,1)S(1)}, bf16[2,4,16,256]{3,2,1,0:T(8,128)(2,1)}, u32[]{:S(2)}) %copy-start.2) | copy-done | bytes 65560
  3.2 0.0 copy-start.3
  3.2 0.8 %copy-done.3 = bf16[2,4,16,256]{3,2,1,0:T(8,128)(2,1)S(1)} copy-done((bf16[2,4,16,256]{3,2,1,0:T(8,128)(2,1)S(1)}, bf16[2,4,16,256]{3,2,1,0:T(8,128)(2,1)}, u32[]{:S(2)}) %copy-start.3) | copy-done | bytes 65560
  4.0 0.0 copy-start.4
  4.0 0.7 %copy-done.4 = bf16[27,256]{1,0:T(8,128)(2,1)S(1)} copy-done((bf16[27,256]{1,0:T(8,128)(2,1)S(1)}, bf16[27,256]{1,0:T(8,128)(2,1)}, u32[]{:S(2)}) %copy-start.4) | copy-done | bytes 13848
  4.7 0.0 copy-start.5
  4.7 0.7 %copy-done.5 = s32[1,1,2]{2,1,0:T(1,128)S(1)} copy-done((s32[1,1,2]{2,1,0:T(1,128)S(1)}, s32[1,1,2]{2,1,0:T(1,128)}, u32[]{:S(2)}) %copy-start.5) | copy-done | bytes 32
  5.4 43.0 %shard_map.93 = (bf16[2,4,16,256]{3,2,1,0:T(8,128)(2,1)S(1)}, bf16[2,4,16,256]{3,2,1,0:T(8,128)(2,1)S(1)}, bf16[2,4,16,256]{3,2,1,0:T(8,128)(2,1)S(1)}, f32[27,256]{1,0:T(8,128)S(1)}) custom-call(bf16[2,4,16,256]{3,2,1,0:T(8,128)(2,1)S(1)} %copy-done, bf16[2,4,16,256]{3,2,1,0:T(8,128)(2,1)S(1)} %copy-done.1, bf16[2,4,16,256]{3,2,1,0:T(8,128)(2,1)S(1)} %copy-done.2, ...), custom_call_target="tpu_custom_call" | custom-call | tf_op jit(solution)/shard_map/pallas_call | solution.py:461
  48.4 0.6 %copy.14 = bf16[2,4,16,256]{3,2,1,0:T(8,128)(2,1)} copy(bf16[2,4,16,256]{3,2,1,0:T(8,128)(2,1)S(1)} %get-tuple-element.8) | data formatting | bytes 131072
  49.0 0.6 %copy.15 = bf16[2,4,16,256]{3,2,1,0:T(8,128)(2,1)} copy(bf16[2,4,16,256]{3,2,1,0:T(8,128)(2,1)S(1)} %get-tuple-element.9) | data formatting | bytes 131072
  49.7 0.6 %copy.16 = bf16[2,4,16,256]{3,2,1,0:T(8,128)(2,1)} copy(bf16[2,4,16,256]{3,2,1,0:T(8,128)(2,1)S(1)} %get-tuple-element.10) | data formatting | bytes 131072
  50.3 0.6 %copy.17 = f32[27,256]{1,0:T(8,128)} copy(f32[27,256]{1,0:T(8,128)S(1)} %get-tuple-element.11) | data formatting | bytes 55296
Async XLA Ops:
  0.6 0.8 %copy-start = (bf16[2,4,16,256]{3,2,1,0:T(8,128)(2,1)S(1)}, bf16[2,4,16,256]{3,2,1,0:T(8,128)(2,1)}, u32[]{:S(2)}) copy-start(bf16[2,4,16,256]{3,2,1,0:T(8,128)(2,1)} %q_ref.1) | copy-start | bytes 196612
  1.5 0.8 %copy-start.1 = (bf16[2,4,16,256]{3,2,1,0:T(8,128)(2,1)S(1)}, bf16[2,4,16,256]{3,2,1,0:T(8,128)(2,1)}, u32[]{:S(2)}) copy-start(bf16[2,4,16,256]{3,2,1,0:T(8,128)(2,1)} %k_ref.1) | copy-start | bytes 196612
  2.3 0.8 %copy-start.2 = (bf16[2,4,16,256]{3,2,1,0:T(8,128)(2,1)S(1)}, bf16[2,4,16,256]{3,2,1,0:T(8,128)(2,1)}, u32[]{:S(2)}) copy-start(bf16[2,4,16,256]{3,2,1,0:T(8,128)(2,1)} %v_ref.1) | copy-start | bytes 196612
  3.2 0.8 %copy-start.3 = (bf16[2,4,16,256]{3,2,1,0:T(8,128)(2,1)S(1)}, bf16[2,4,16,256]{3,2,1,0:T(8,128)(2,1)}, u32[]{:S(2)}) copy-start(bf16[2,4,16,256]{3,2,1,0:T(8,128)(2,1)} %g_ref.1) | copy-start | bytes 196612
  4.0 0.7 %copy-start.4 = (bf16[27,256]{1,0:T(8,128)(2,1)S(1)}, bf16[27,256]{1,0:T(8,128)(2,1)}, u32[]{:S(2)}) copy-start(bf16[27,256]{1,0:T(8,128)(2,1)} %w_ref.1) | copy-start | bytes 41476
  4.7 0.7 %copy-start.5 = (s32[1,1,2]{2,1,0:T(1,128)S(1)}, s32[1,1,2]{2,1,0:T(1,128)}, u32[]{:S(2)}) copy-start(s32[1,1,2]{2,1,0:T(1,128)} %keep_ref.1) | copy-start | bytes 28

commit v2 on v1

v2 whole, which is shorter than its diff:
```python
from functools import partial

import jax
import jax.numpy as jnp
from jax import lax
from jax.experimental import pallas as pl
from jax.experimental.pallas import tpu as pltpu
from jax.sharding import PartitionSpec as P

HEAD = 32
BX = 8
LANES = 128
GROUP_HEADS = LANES // HEAD
DEAD = 4.0
LOG2E = 1.4426950408889634
MESH = pl.DeviceIdType.MESH
F32 = jnp.float32
BF16 = jnp.bfloat16
SIDES = ("zm", "zp", "ym", "yp")
CORNERS = (("zm", "ym"), ("zm", "yp"), ("zp", "ym"), ("zp", "yp"))


def rounds_of(sections, rows):
    if sections == 16 and rows == 16:
        return [[("gz", 4, 4), ("gy", 8, 2)], [("gz", 1, 4), ("gy", 2, 4)]]
    return [[("gz", 1, sections)], [("gy", 2, rows // 2)]]


def kernel(
    sections,
    rows_n,
    depth,
    rows,
    cols,
    q_hbm,
    k_hbm,
    v_hbm,
    g_hbm,
    w_hbm,
    keep_hbm,
    gq_ref,
    gk_ref,
    gv_ref,
    cg_ref,
    q_ref,
    g_ref,
    w_ref,
    keep_ref,
    ext_k,
    ext_v,
    near_v,
    acc,
    qm,
    gm,
    shifted,
    filt,
    eights,
    mask,
    part_y,
    got_y,
    part_z,
    got_z,
    halves,
    terms,
    load_sem,
    halo_send,
    halo_recv,
    near_send,
    near_recv,
    py_send,
    py_recv,
    pz_send,
    pz_recv,
    half_send,
    half_recv,
    sum_send,
    sum_recv,
):
    groups = acc.shape[0]
    tokens = depth * rows * cols
    place = {"gz": lax.axis_index("gz"), "gy": lax.axis_index("gy")}
    gz, gy = place["gz"], place["gy"]
    has = {
        "zm": gz > 0,
        "zp": gz < sections - 1,
        "ym": gy > 0,
        "yp": gy < rows_n - 1,
    }
    shift = {"zm": -1, "zp": 1, "ym": -1, "yp": 1}
    core = lax.rem(gy, 2)
    partner = (gz, gy + 1 - 2 * core)
    sum_rounds = rounds_of(sections, rows_n)

    def both(names):
        found = has[names[0]]
        for name in names[1:]:
            found = jnp.logical_and(found, has[name])
        return found

    def device(names):
        to = dict(place)
        for name in names:
            axis = "g" + name[0]
            to[axis] = to[axis] + shift[name]
        return (to["gz"], to["gy"])

    def digit(spec):
        axis, stride, count = spec
        return lax.rem(lax.div(place[axis], stride), count)

    def member_of(digits):
        m = 0
        for spec in digits:
            m = m * spec[2] + digit(spec)
        return m

    def peer(digits, m):
        out = dict(place)
        for spec in reversed(digits):
            axis, stride, count = spec
            want = lax.rem(m, count)
            m = lax.div(m, count)
            out[axis] = out[axis] + (want - digit(spec)) * stride
        return (out["gz"], out["gy"])

    def size_of(digits):
        n = 1
        for spec in digits:
            n *= spec[2]
        return n

    def load(source, target, sem):
        return pltpu.make_async_copy(source, target, load_sem.at[sem])

    z_own, z_first, z_last = pl.ds(2, depth), pl.ds(0, 2), pl.ds(2 + depth, 2)
    inner, low, high = pl.ds(2, rows), pl.ds(2, 2), pl.ds(rows, 2)
    y_first, y_last = pl.ds(0, 2), pl.ds(2 + rows, 2)
    parts = [slice(g * LANES, (g + 1) * LANES) for g in range(groups)]
    loads = [load(keep_hbm, keep_ref, 0)]
    loads += [load(v_hbm.at[:, :, :, parts[g]], ext_v.at[g, z_own, inner], 1 + g) for g in range(groups)]
    loads += [load(k_hbm.at[:, :, :, parts[g]], ext_k.at[g, z_own, inner], 3 + g) for g in range(groups)]
    loads += [load(g_hbm, g_ref, 5), load(q_hbm, q_ref, 6), load(w_hbm, w_ref, 7)]
    for copy in loads:
        copy.start()

    barrier = pltpu.get_barrier_semaphore()
    expected = 0
    for names in tuple((side,) for side in SIDES) + CORNERS:

        @pl.when(both(names))
        def _(names=names):
            pl.semaphore_signal(barrier, inc=1, device_id=device(names), device_id_type=MESH)

        expected = expected + both(names).astype(jnp.int32)
    pl.semaphore_signal(barrier, inc=1, device_id=partner, device_id_type=MESH)
    expected = expected + 1
    for digits in sum_rounds:
        n = size_of(digits)
        me = member_of(digits)
        for step in range(1, n):
            pl.semaphore_signal(
                barrier, inc=1, device_id=peer(digits, lax.rem(me + step, n)), device_id_type=MESH
            )
        expected = expected + (n - 1)

    loads[0].wait()
    keep_low = keep_ref[0, 0, 0].astype(F32)
    keep_high = keep_ref[0, 0, 1].astype(F32)
    row_x = lax.broadcasted_iota(jnp.int32, (cols, LANES), 0)
    row_keep = jnp.where(row_x < BX, keep_low, keep_high)
    lane = lax.broadcasted_iota(jnp.int32, (1, LANES), 1)
    lane_x = lane % cols
    lane_keep = jnp.where(lane_x < BX, keep_low, keep_high)
    lane_head = lane // HEAD

    for g in range(groups):
        loads[1 + g].wait()
    for g in range(groups):
        loads[3 + g].wait()
        own = ext_k[g, 2 : 2 + depth, 2 : 2 + rows].astype(F32)
        ext_k[g, 2 : 2 + depth, 2 : 2 + rows] = jnp.where(row_keep > 0.5, own, DEAD).astype(BF16)

    pl.semaphore_wait(barrier, expected)

    kinds = [ext_v] + [ext_k.at[g] for g in range(groups)]
    halo = [
        (("zp",), (z_own, inner), (z_first, inner), ("zm",)),
        (("zm",), (z_own, inner), (z_last, inner), ("zp",)),
        (("yp",), (z_own, high), (z_own, y_first), ("ym",)),
        (("ym",), (z_own, low), (z_own, y_last), ("yp",)),
        (("yp", "zm"), (z_first, high), (z_first, y_first), ("ym", "zm")),
        (("ym", "zm"), (z_first, low), (z_first, y_last), ("yp", "zm")),
        (("yp", "zp"), (z_last, high), (z_last, y_first), ("ym", "zp")),
        (("ym", "zp"), (z_last, low), (z_last, y_last), ("yp", "zp")),
    ]

    def halo_copy(kind, slot):
        to, (sz, sy), (dz, dy), _ = halo[slot]
        ref = kinds[kind]
        src, dst = (ref.at[:, sz, sy], ref.at[:, dz, dy]) if kind == 0 else (ref.at[sz, sy], ref.at[dz, dy])
        return pltpu.make_async_remote_copy(
            src_ref=src,
            dst_ref=dst,
            send_sem=halo_send.at[kind, slot],
            recv_sem=halo_recv.at[kind, slot],
            device_id=device(to[:1]),
            device_id_type=MESH,
        )

    def halo_start(kind, slots):
        for slot in slots:

            @pl.when(both(halo[slot][0]))
            def _(slot=slot):
                halo_copy(kind, slot).start()

    def halo_sent(kind, slots):
        for slot in slots:

            @pl.when(both(halo[slot][0]))
            def _(slot=slot):
                halo_copy(kind, slot).wait_send()

    def halo_got(kind, slots):
        for slot in slots:

            @pl.when(both(halo[slot][3]))
            def _(slot=slot):
                halo_copy(kind, slot).wait_recv()

    def near_copy(corner):
        up_z, up_y = CORNERS[corner][0] == "zm", CORNERS[corner][1] == "ym"
        return pltpu.make_async_remote_copy(
            src_ref=ext_v.at[:, 1 + depth if up_z else 2, 1 + rows if up_y else 2],
            dst_ref=near_v.at[:, 0 if up_z else 1 + depth, 0 if up_y else 1 + rows],
            send_sem=near_send.at[corner],
            recv_sem=near_recv.at[corner],
            device_id=device(("zp" if up_z else "zm", "yp" if up_y else "ym")),
            device_id_type=MESH,
        )

    def opposite(corner):
        return tuple(name[0] + ("p" if name[1] == "m" else "m") for name in CORNERS[corner])

    halo_start(0, (0, 1, 2, 3))
    for corner in range(4):

        @pl.when(both(opposite(corner)))
        def _(corner=corner):
            near_copy(corner).start()

    for g in range(groups):
        halo_start(1 + g, (0, 1, 2, 3))

    for side, where in (
        ("zm", (slice(None), z_first)),
        ("zp", (slice(None), z_last)),
        ("ym", (slice(None), slice(None), y_first)),
        ("yp", (slice(None), slice(None), y_last)),
    ):

        @pl.when(jnp.logical_not(has[side]))
        def _(side=side, where=where):
            shape = ext_k[where].shape
            ext_k[where] = jnp.full(shape, DEAD, BF16)
            ext_v[where] = jnp.zeros(shape, BF16)
            got = got_z if side[0] == "z" else got_y
            slot = 0 if side[1] == "m" else 1
            got[:, slot] = jnp.zeros(got[:, slot].shape, BF16)

    for corner in range(4):

        @pl.when(jnp.logical_not(both(CORNERS[corner])))
        def _(corner=corner):
            z = 0 if CORNERS[corner][0] == "zm" else 1 + depth
            y = 0 if CORNERS[corner][1] == "ym" else 1 + rows
            near_v[:, z, y] = jnp.zeros((groups, cols, LANES), BF16)

    for copy in loads[5:]:
        copy.wait()
    for o in range(27):
        filt[o] = jnp.broadcast_to(w_ref[o : o + 1].astype(F32), filt.shape[1:])

    def own_row(y, carry):
        for g in range(groups):
            part = parts[g]
            for z in range(depth):
                q_row = q_ref[z, y, :, part].astype(F32)
                g_row = g_ref[z, y, :, part].astype(F32)
                for h in range(GROUP_HEADS):
                    at = pl.ds((z * GROUP_HEADS + h) * cols, cols)
                    mine = lane_head == h
                    qm[g, y, at] = jnp.where(mine, q_row, 0.0).astype(BF16)
                    gm[g, y, at] = jnp.where(mine, g_row, 0.0).astype(BF16)
                none = jnp.zeros((1, LANES), F32)
                shifted[g, 0, z, y] = jnp.concatenate([g_row[1:], none], axis=0)
                shifted[g, 1, z, y] = g_row
                shifted[g, 2, z, y] = jnp.concatenate([none, g_row[:-1]], axis=0)
        return carry

    lax.fori_loop(0, rows, own_row, 0)
    acc[...] = jnp.zeros(acc.shape, F32)
    eights[27:] = jnp.zeros((5, 8, eights.shape[2]), F32)
    octets = (depth * rows * cols // 8, 8, LANES)
    whole = (depth, rows, cols, LANES)

    def filter_values(i, carry):
        oz, oy = lax.div(i, 3), lax.rem(i, 3)
        for g in range(groups):
            total = acc[g, 1, pl.ds(1 + oz, depth), pl.ds(1 + oy, rows)].reshape(octets)
            for ox in range(3):
                total = total + filt[3 * i + ox, :, parts[g]] * shifted[g, ox].reshape(octets)
            acc[g, 1, pl.ds(1 + oz, depth), pl.ds(1 + oy, rows)] = total.reshape(whole)
        return carry

    band = jnp.abs(row_x - lane_x) <= 2
    half = lax.broadcasted_iota(jnp.int32, (cols, LANES), 1) // (GROUP_HEADS * cols)

    def make_mask():
        for z in range(depth + 4):
            reach = band
            for own in range(depth):
                if not own <= z <= own + 4:
                    reach = jnp.logical_and(reach, half != own)
            live = jnp.where(reach, 1.0, 0.0)
            mask[z] = jnp.where(ext_k[0, z].astype(F32) < 3.0, live, 0.0)

    scaling = HEAD**-0.5
    keys_n = (depth + 4) * 5 * cols
    head_row = lax.broadcasted_iota(jnp.int32, (depth * GROUP_HEADS * cols, LANES), 0)
    head_row = (head_row // cols) % GROUP_HEADS
    own_head = head_row == lax.broadcasted_iota(jnp.int32, head_row.shape, 1) // HEAD

    def attend(g):
        def row(y, carry):
            near = pl.ds(y, 5)
            keys = ext_k[g, :, near].reshape(keys_n, LANES)
            values = ext_v[g, :, near].reshape(keys_n, LANES)
            queries, grads = qm[g, y], gm[g, y]
            nt = (((1,), (1,)), ((), ()))
            tn = (((0,), (0,)), ((), ()))
            scores = lax.dot_general(keys, queries, nt, preferred_element_type=F32)
            weights = jnp.exp2(scores * (scaling * LOG2E)) * mask[:, near].reshape(keys_n, LANES)
            totals = jnp.sum(weights, axis=0, keepdims=True) + (1.0 - lane_keep)
            probs = weights * (lane_keep / totals)
            probs_low = probs.astype(BF16)
            dprobs = lax.dot_general(values, grads, nt, preferred_element_type=F32)
            deltas = jnp.sum(probs_low.astype(F32) * dprobs, axis=0, keepdims=True)
            dscores = (scaling * probs * (dprobs - deltas)).astype(BF16)
            shape = (depth + 4, 5, cols, LANES)
            acc[g, 1, :, near] += jnp.dot(
                probs_low, grads, preferred_element_type=F32
            ).reshape(shape)
            acc[g, 0, :, near] += jnp.dot(
                dscores, queries, preferred_element_type=F32
            ).reshape(shape)
            dq = lax.dot_general(dscores, keys, tn, preferred_element_type=F32)
            dq = jnp.where(own_head, dq, 0.0).reshape(depth, GROUP_HEADS, cols, LANES)
            gq_ref[:, pl.ds(y, 1), :, parts[g]] = jnp.sum(dq, axis=1)[:, None].astype(BF16)
            return carry

        return row

    def part_copy(g, stage, slot):
        if stage == "y":
            src, dst, sends, recvs = part_y, got_y, py_send, py_recv
        else:
            src, dst, sends, recvs = part_z, got_z, pz_send, pz_recv
        to = stage + ("p" if slot == 0 else "m")
        source = stage + ("m" if slot == 0 else "p")
        copy = pltpu.make_async_remote_copy(
            src_ref=src.at[g, slot],
            dst_ref=dst.at[g, slot],
            send_sem=sends.at[g, slot],
            recv_sem=recvs.at[g, slot],
            device_id=device((to,)),
            device_id_type=MESH,
        )
        return to, source, copy

    def part_start(g, stage, slot):
        to, _, copy = part_copy(g, stage, slot)

        @pl.when(has[to])
        def _():
            copy.start()

    def part_got(g, stage, slot):
        _, source, copy = part_copy(g, stage, slot)

        @pl.when(has[source])
        def _():
            copy.wait_recv()

    def part_sent(g, stage, slot):
        to, _, copy = part_copy(g, stage, slot)

        @pl.when(has[to])
        def _():
            copy.wait_send()

    def send_rows(g, slot):
        at = 2 + rows if slot == 0 else 0
        part_y[g, slot] = acc[g, :, :, at : at + 2].astype(BF16)
        part_start(g, "y", slot)

    def send_sections(g):
        part_got(g, "y", 0)
        part_got(g, "y", 1)
        acc[g, :, :, 2:4] += got_y[g, 0].astype(F32)
        acc[g, :, :, rows : rows + 2] += got_y[g, 1].astype(F32)
        for slot in range(2):
            at = 2 + depth if slot == 0 else 0
            part_z[g, slot] = acc[g, :, at : at + 2, 2 : 2 + rows].astype(BF16)
            part_start(g, "z", slot)

    def finish(g):
        part_got(g, "z", 0)
        part_got(g, "z", 1)
        for kind, out in ((0, gk_ref), (1, gv_ref)):
            total = acc[g, kind, 2 : 2 + depth, 2 : 2 + rows]
            total = total + got_z[g, 0, kind].astype(F32) + got_z[g, 1, kind].astype(F32)
            out[:, :, :, parts[g]] = total.astype(BF16)

    def filter_terms():
        near_v[:, 1 : 1 + depth, 1 : 1 + rows] = ext_v[:, 2 : 2 + depth, 2 : 2 + rows]
        near_v[:, 0, 1 : 1 + rows] = ext_v[:, 1, 2 : 2 + rows]
        near_v[:, 1 + depth, 1 : 1 + rows] = ext_v[:, 2 + depth, 2 : 2 + rows]
        near_v[:, 1 : 1 + depth, 0] = ext_v[:, 2 : 2 + depth, 1]
        near_v[:, 1 : 1 + depth, 1 + rows] = ext_v[:, 2 : 2 + depth, 2 + rows]

        def one(i, carry):
            oz, oy = lax.div(i, 3), lax.rem(i, 3)
            for g in range(groups):
                near = near_v[g, pl.ds(oz, depth), pl.ds(oy, rows)].astype(F32)
                for ox in range(3):
                    product = (near * shifted[g, ox]).reshape(octets)
                    eights[3 * i + ox, :, parts[g]] = jnp.sum(product, axis=0)
            return carry

        lax.fori_loop(0, 9, one, 0)

    def half_copy(stage):
        slot = (1 - core, 2) if stage == 0 else (core, 3)
        return pltpu.make_async_remote_copy(
            src_ref=halves.at[slot[0]],
            dst_ref=halves.at[slot[1]],
            send_sem=half_send.at[stage],
            recv_sem=half_recv.at[stage],
            device_id=partner,
            device_id_type=MESH,
        )

    def sum_begin():
        total = jnp.sum(eights[...], axis=1)
        for g in range(groups):
            halves[g] = total[:, parts[g]]
        half_copy(0).start()

    def sum_copy(r, step):
        digits = sum_rounds[r]
        me = member_of(digits)
        return pltpu.make_async_remote_copy(
            src_ref=terms.at[r, me],
            dst_ref=terms.at[r, me],
            send_sem=sum_send.at[r],
            recv_sem=sum_recv.at[r],
            device_id=peer(digits, lax.rem(me + step, size_of(digits))),
            device_id_type=MESH,
        )

    def sum_all(r):
        n = size_of(sum_rounds[r])
        return pltpu.make_async_remote_copy(
            src_ref=terms.at[r, pl.ds(0, n - 1)],
            dst_ref=terms.at[r, pl.ds(0, n - 1)],
            send_sem=sum_send.at[r],
            recv_sem=sum_recv.at[r],
            device_id=partner,
            device_id_type=MESH,
        )

    def sum_start(r, total):
        terms[r, member_of(sum_rounds[r])] = total.astype(BF16)
        for step in range(1, size_of(sum_rounds[r])):
            sum_copy(r, step).start()

    def sum_first():
        half_copy(0).wait_recv()
        sum_start(0, halves[core] + halves[2])

    def sum_got(r):
        sum_all(r).wait_recv()
        total = terms[r, 0].astype(F32)
        for m in range(1, size_of(sum_rounds[r])):
            total = total + terms[r, m].astype(F32)
        return total

    def sum_second():
        sum_start(1, sum_got(0))

    def sum_third():
        total = sum_got(1) * ((tokens * sections * rows_n) ** -0.5)
        half_copy(0).wait_send()
        halves[core] = total
        half_copy(1).start()

    def sum_last():
        half_copy(1).wait_recv()
        mine, other = halves[core, 0:27], halves[3, 0:27]
        cg_ref[:, parts[0]] = jnp.where(core == 0, mine, other)
        cg_ref[:, parts[1]] = jnp.where(core == 0, other, mine)

    z_slots, y_slots, m_relays, p_relays = (0, 1), (2, 3), (4, 5), (6, 7)

    def relay(kind):
        halo_got(kind, z_slots[:1])
        halo_start(kind, m_relays)
        halo_got(kind, z_slots[1:])
        halo_start(kind, p_relays)

    lax.fori_loop(0, 9, filter_values, 0)
    relay(0)
    halo_got(0, y_slots)
    for corner in range(4):

        @pl.when(both(CORNERS[corner]))
        def _(corner=corner):
            near_copy(corner).wait_recv()

    filter_terms()
    sum_begin()
    relay(1)
    sum_first()
    relay(2)
    halo_got(0, m_relays + p_relays)
    halo_got(1, y_slots + m_relays + p_relays)
    make_mask()
    lax.fori_loop(0, 2, attend(0), 0)
    send_rows(0, 1)
    lax.fori_loop(2, rows, attend(0), 0)
    send_rows(0, 0)
    halo_got(2, y_slots + m_relays + p_relays)
    lax.fori_loop(0, 2, attend(1), 0)
    send_rows(1, 1)
    lax.fori_loop(2, rows, attend(1), 0)
    send_rows(1, 0)
    sum_second()
    send_sections(0)
    send_sections(1)
    for kind in range(3):
        halo_sent(kind, range(8))
    for corner in range(4):

        @pl.when(both(opposite(corner)))
        def _(corner=corner):
            near_copy(corner).wait_send()

    sum_all(0).wait_send()
    sum_third()
    for g in range(groups):
        for slot in range(2):
            part_sent(g, "y", slot)
    finish(0)
    sum_last()
    finish(1)
    for g in range(groups):
        for slot in range(2):
            part_sent(g, "z", slot)
    sum_all(1).wait_send()
    half_copy(1).wait_send()


def write_out(*refs):
    n = len(refs) // 2
    sems = refs[-1]
    copies = [pltpu.make_async_copy(refs[i], refs[n + i], sems.at[i]) for i in range(n)]
    for copy in copies:
        copy.start()
    for copy in copies:
        copy.wait()


def shards(sections, rows_n, queries, keys, values, cotangent, conv_weight, block_keep):
    depth, rows, cols, channels = queries.shape
    groups = channels // LANES
    heads_rows = depth * GROUP_HEADS * cols
    most = max(sections * rows_n // 32, 16)
    big = jax.ShapeDtypeStruct(queries.shape, BF16)
    small = jax.ShapeDtypeStruct(conv_weight.shape, F32)
    vmem = pl.BlockSpec(memory_space=pltpu.VMEM)
    hbm = pl.BlockSpec(memory_space=pltpu.HBM)
    dma = pltpu.SemaphoreType.DMA
    ext = (groups, depth + 4, rows + 4, cols, LANES)
    results = pl.pallas_call(
        partial(kernel, sections, rows_n, depth, rows, cols),
        out_shape=(big, big, big, small),
        in_specs=[hbm] * 6,
        out_specs=(vmem,) * 4,
        scratch_shapes=[
            pltpu.VMEM(queries.shape, BF16),
            pltpu.VMEM(queries.shape, BF16),
            pltpu.VMEM(conv_weight.shape, BF16),
            pltpu.SMEM(block_keep.shape, jnp.int32),
            pltpu.VMEM(ext, BF16),
            pltpu.VMEM(ext, BF16),
            pltpu.VMEM((groups, depth + 2, rows + 2, cols, LANES), BF16),
            pltpu.VMEM((groups, 2, depth + 4, rows + 4, cols, LANES), F32),
            pltpu.VMEM((groups, rows, heads_rows, LANES), BF16),
            pltpu.VMEM((groups, rows, heads_rows, LANES), BF16),
            pltpu.VMEM((groups, 3, depth, rows, cols, LANES), F32),
            pltpu.VMEM((27, 8, channels), F32),
            pltpu.VMEM((32, 8, channels), F32),
            pltpu.VMEM((depth + 4, rows + 4, cols, LANES), F32),
            pltpu.VMEM((groups, 2, 2, depth + 4, 2, cols, LANES), BF16),
            pltpu.VMEM((groups, 2, 2, depth + 4, 2, cols, LANES), BF16),
            pltpu.VMEM((groups, 2, 2, 2, rows, cols, LANES), BF16),
            pltpu.VMEM((groups, 2, 2, 2, rows, cols, LANES), BF16),
            pltpu.VMEM((4, 32, LANES), F32),
            pltpu.VMEM((2, most, 32, LANES), BF16),
            dma((8,)),
            dma((3, 8)),
            dma((3, 8)),
            dma((4,)),
            dma((4,)),
            dma((groups, 2)),
            dma((groups, 2)),
            dma((groups, 2)),
            dma((groups, 2)),
            dma((2,)),
            dma((2,)),
            dma((2,)),
            dma((2,)),
        ],
        compiler_params=pltpu.CompilerParams(
            collective_id=0, has_side_effects=True, vmem_limit_bytes=60 * 1024 * 1024
        ),
    )(queries, keys, values, cotangent, conv_weight, block_keep)
    return pl.pallas_call(
        write_out,
        out_shape=(big, big, big, small),
        in_specs=[vmem] * 4,
        out_specs=(hbm,) * 4,
        scratch_shapes=[dma((4,))],
    )(*results)


def solution(mesh):
    in_specs = (
        P("gz", "gy", None, None),
        P("gz", "gy", None, None),
        P("gz", "gy", None, None),
        P("gz", "gy", None, None),
        P(),
        P("gz", "gy", None),
    )
    out_specs = (
        P("gz", "gy", None, None),
        P("gz", "gy", None, None),
        P("gz", "gy", None, None),
        P(),
    )
    return jax.shard_map(
        partial(shards, mesh.shape["gz"], mesh.shape["gy"]),
        mesh=mesh,
        in_specs=in_specs,
        out_specs=out_specs,
        check_vma=False,
    )
```

time: 51.2 us -> 38.6 us (0.75)
  the two profiles are of different devices: /device:TPU:4 before, /device:TPU:31 now
where the time goes in v2:
time: 38.6 us; the launch traced here: 38.4 us
  Pallas kernels  37.8 us (98%)
  between operations  0.64 us (2%)
    pallas_call x1, Pallas kernels, shards(): pl.pallas_call(partial(kernel, sections, rows_n, depth, rows, cols), out_...  36.1 us
    pallas_call x1, Pallas kernels, shards(): pl.pallas_call(write_out, out_shape=(big, big, big, small), in_specs=[vme...  1.62 us

profile of v2, /device:TPU:31, one launch (start us, length us, event | category | flops | bytes accessed | tf_op | source)
XLA Modules:
  0.0 38.4 jit_solution(933482335585849328)
XLA Ops:
  0.6 36.1 %shard_map.93 = (bf16[2,4,16,256]{3,2,1,0:T(8,128)(2,1)}, bf16[2,4,16,256]{3,2,1,0:T(8,128)(2,1)}, bf16[2,4,16,256]{3,2,1,0:T(8,128)(2,1)}, f32[27,256]{1,0:T(8,128)}) custom-call(bf16[2,4,16,256]{3,2,1,0:T(8,128)(2,1)} %q_hbm.1, bf16[2,4,16,256]{3,2,1,0:T(8,128)(2,1)} %k_hbm.1, bf16[2,4,16,256]{3,2,1,0:T(8,128)(2,1)} %v_hbm.1, ...), custom_call_target="tpu_custom_call" | custom-call | tf_op jit(solution)/shard_map/pallas_call | solution.py:595
  36.8 1.6 %shard_map.94 = (bf16[2,4,16,256]{3,2,1,0:T(8,128)(2,1)}, bf16[2,4,16,256]{3,2,1,0:T(8,128)(2,1)}, bf16[2,4,16,256]{3,2,1,0:T(8,128)(2,1)}, f32[27,256]{1,0:T(8,128)}) custom-call(bf16[2,4,16,256]{3,2,1,0:T(8,128)(2,1)} %get-tuple-element.8.refs_0_, bf16[2,4,16,256]{3,2,1,0:T(8,128)(2,1)} %get-tuple-element.9.refs_1_, ...), custom_call_target="tpu_custom_call" | custom-call | tf_op jit(solution)/shard_map/pallas_call | solution.py:639

commit v3 on v2

--- a/solution.py
+++ b/solution.py
@@ -13,6 +13,7 @@
 GROUP_HEADS = LANES // HEAD
 DEAD = 4.0
 LOG2E = 1.4426950408889634
+HALO_COPIES = 24
 MESH = pl.DeviceIdType.MESH
 F32 = jnp.float32
 BF16 = jnp.bfloat16
@@ -46,8 +47,7 @@
     g_ref,
     w_ref,
     keep_ref,
-    ext_k,
-    ext_v,
+    ext,
     near_v,
     acc,
     qm,
@@ -114,14 +114,21 @@
             m = m * spec[2] + digit(spec)
         return m
 
-    def peer(digits, m):
+    def peer(digits, moves):
         out = dict(place)
-        for spec in reversed(digits):
+        for spec, move in zip(digits, moves):
             axis, stride, count = spec
-            want = lax.rem(m, count)
-            m = lax.div(m, count)
-            out[axis] = out[axis] + (want - digit(spec)) * stride
+            own = digit(spec)
+            out[axis] = out[axis] + (lax.rem(own + move, count) - own) * stride
         return (out["gz"], out["gy"])
+
+    def moves_of(digits):
+        moves = [()]
+        for _, _, count in digits:
+            moves = [m + (k,) for m in moves for k in range(count)]
+        weight = lambda m: sum(min(k, spec[2] - k) * spec[3] for k, spec in zip(m, hops))
+        hops = [spec + (2 if spec[:2] == ("gz", 4) else 1,) for spec in digits]
+        return sorted((m for m in moves if any(m)), key=lambda m: (-weight(m), m))
 
     def size_of(digits):
         n = 1
@@ -137,8 +144,8 @@
     y_first, y_last = pl.ds(0, 2), pl.ds(2 + rows, 2)
     parts = [slice(g * LANES, (g + 1) * LANES) for g in range(groups)]
     loads = [load(keep_hbm, keep_ref, 0)]
-    loads += [load(v_hbm.at[:, :, :, parts[g]], ext_v.at[g, z_own, inner], 1 + g) for g in range(groups)]
-    loads += [load(k_hbm.at[:, :, :, parts[g]], ext_k.at[g, z_own, inner], 3 + g) for g in range(groups)]
+    loads += [load(v_hbm.at[:, :, :, parts[g]], ext.at[g, 1, z_own, inner], 1 + g) for g in range(groups)]
+    loads += [load(k_hbm.at[:, :, :, parts[g]], ext.at[g, 0, z_own, inner], 3 + g) for g in range(groups)]
     loads += [load(g_hbm, g_ref, 5), load(q_hbm, q_ref, 6), load(w_hbm, w_ref, 7)]
     for copy in loads:
         copy.start()
@@ -155,13 +162,9 @@
     pl.semaphore_signal(barrier, inc=1, device_id=partner, device_id_type=MESH)
     expected = expected + 1
     for digits in sum_rounds:
-        n = size_of(digits)
-        me = member_of(digits)
-        for step in range(1, n):
-            pl.semaphore_signal(
-                barrier, inc=1, device_id=peer(digits, lax.rem(me + step, n)), device_id_type=MESH
-            )
-        expected = expected + (n - 1)
+        for moves in moves_of(digits):
+            pl.semaphore_signal(barrier, inc=1, device_id=peer(digits, moves), device_id_type=MESH)
+        expected = expected + (size_of(digits) - 1)
 
     loads[0].wait()
     keep_low = keep_ref[0, 0, 0].astype(F32)
@@ -175,63 +178,80 @@
 
     for g in range(groups):
         loads[1 + g].wait()
+    pl.semaphore_wait(barrier, expected)
+
+    every = pl.ds(0, groups)
+    border = {"zp": 1 + depth, "zm": 2}
+    behind = {"zp": 2, "zm": 1 + depth}
+    far = {"zp": -depth, "zm": depth}
+
+    def along_z(name, to):
+        if name == "near":
+            return (every, 1, pl.ds(border[to], 1), inner), (every, 1, pl.ds(border[to] + far[to], 1), inner)
+        g = int(name[-1])
+        if name[0] == "v":
+            return (g, 1, pl.ds(behind[to], 1), inner), (g, 1, pl.ds(behind[to] + far[to], 1), inner)
+        return (g, 0, z_own, inner), (g, 0, z_first if to == "zp" else z_last, inner)
+
+    halo = []
+    index = {}
+    for name in ["near"] + [kind + str(g) for g in range(groups) for kind in ("v", "k")]:
+        for to, source in (("zp", "zm"), ("zm", "zp")):
+            src, dst = along_z(name, to)
+            index[name, source] = len(halo)
+            halo.append(((to,), src, dst, (source,)))
+    for name, at in [("vy", (every, 1))] + [("ky" + str(g), (g, 0)) for g in range(groups)]:
+        index[name, "ym"] = len(halo)
+        halo.append((("yp",), at + (z_own, high), at + (z_own, y_first), ("ym",)))
+        index[name, "yp"] = len(halo)
+        halo.append((("ym",), at + (z_own, low), at + (z_own, y_last), ("yp",)))
     for g in range(groups):
-        loads[3 + g].wait()
-        own = ext_k[g, 2 : 2 + depth, 2 : 2 + rows].astype(F32)
-        ext_k[g, 2 : 2 + depth, 2 : 2 + rows] = jnp.where(row_keep > 0.5, own, DEAD).astype(BF16)
-
-    pl.semaphore_wait(barrier, expected)
-
-    kinds = [ext_v] + [ext_k.at[g] for g in range(groups)]
-    halo = [
-        (("zp",), (z_own, inner), (z_first, inner), ("zm",)),
-        (("zm",), (z_own, inner), (z_last, inner), ("zp",)),
-        (("yp",), (z_own, high), (z_own, y_first), ("ym",)),
-        (("ym",), (z_own, low), (z_own, y_last), ("yp",)),
-        (("yp", "zm"), (z_first, high), (z_first, y_first), ("ym", "zm")),
-        (("ym", "zm"), (z_first, low), (z_first, y_last), ("yp", "zm")),
-        (("yp", "zp"), (z_last, high), (z_last, y_first), ("ym", "zp")),
-        (("ym", "zp"), (z_last, low), (z_last, y_last), ("yp", "zp")),
-    ]
-
-    def halo_copy(kind, slot):
-        to, (sz, sy), (dz, dy), _ = halo[slot]
-        ref = kinds[kind]
-        src, dst = (ref.at[:, sz, sy], ref.at[:, dz, dy]) if kind == 0 else (ref.at[sz, sy], ref.at[dz, dy])
+        kv = pl.ds(0, 2)
+        for source, z in (("zm", z_first), ("zp", z_last)):
+            index["c", g, "ym", source] = len(halo)
+            halo.append((("yp", source), (g, kv, z, high), (g, kv, z, y_first), ("ym", source)))
+            index["c", g, "yp", source] = len(halo)
+            halo.append((("ym", source), (g, kv, z, low), (g, kv, z, y_last), ("yp", source)))
+    assert len(halo) == HALO_COPIES
+
+    def halo_copy(slot):
+        to, src, dst, _ = halo[slot]
         return pltpu.make_async_remote_copy(
-            src_ref=src,
-            dst_ref=dst,
-            send_sem=halo_send.at[kind, slot],
-            recv_sem=halo_recv.at[kind, slot],
+            src_ref=ext.at[src],
+            dst_ref=ext.at[dst],
+            send_sem=halo_send.at[slot],
+            recv_sem=halo_recv.at[slot],
             device_id=device(to[:1]),
             device_id_type=MESH,
         )
 
-    def halo_start(kind, slots):
-        for slot in slots:
+    def halo_start(*names):
+        for name in names:
+            slot = index[name]
 
             @pl.when(both(halo[slot][0]))
             def _(slot=slot):
-                halo_copy(kind, slot).start()
-
-    def halo_sent(kind, slots):
-        for slot in slots:
+                halo_copy(slot).start()
+
+    def halo_got(*names):
+        for name in names:
+            slot = index[name]
+
+            @pl.when(both(halo[slot][3]))
+            def _(slot=slot):
+                halo_copy(slot).wait_recv()
+
+    def halo_sent():
+        for slot in range(len(halo)):
 
             @pl.when(both(halo[slot][0]))
             def _(slot=slot):
-                halo_copy(kind, slot).wait_send()
-
-    def halo_got(kind, slots):
-        for slot in slots:
-
-            @pl.when(both(halo[slot][3]))
-            def _(slot=slot):
-                halo_copy(kind, slot).wait_recv()
+                halo_copy(slot).wait_send()
 
     def near_copy(corner):
         up_z, up_y = CORNERS[corner][0] == "zm", CORNERS[corner][1] == "ym"
         return pltpu.make_async_remote_copy(
-            src_ref=ext_v.at[:, 1 + depth if up_z else 2, 1 + rows if up_y else 2],
+            src_ref=ext.at[:, 1, 1 + depth if up_z else 2, 1 + rows if up_y else 2],
             dst_ref=near_v.at[:, 0 if up_z else 1 + depth, 0 if up_y else 1 + rows],
             send_sem=near_send.at[corner],
             recv_sem=near_recv.at[corner],
@@ -242,7 +262,7 @@
     def opposite(corner):
         return tuple(name[0] + ("p" if name[1] == "m" else "m") for name in CORNERS[corner])
 
-    halo_start(0, (0, 1, 2, 3))
+    halo_start(("near", "zm"), ("near", "zp"), ("vy", "ym"), ("vy", "yp"))
     for corner in range(4):
 
         @pl.when(both(opposite(corner)))
@@ -250,20 +270,27 @@
             near_copy(corner).start()
 
     for g in range(groups):
-        halo_start(1 + g, (0, 1, 2, 3))
+        loads[3 + g].wait()
+        own = ext[g, 0, 2 : 2 + depth, 2 : 2 + rows].astype(F32)
+        ext[g, 0, 2 : 2 + depth, 2 : 2 + rows] = jnp.where(row_keep > 0.5, own, DEAD).astype(BF16)
+
+    for g in range(groups):
+        for kind in ("v", "k"):
+            halo_start((kind + str(g), "zm"), (kind + str(g), "zp"))
+        halo_start(("ky" + str(g), "ym"), ("ky" + str(g), "yp"))
 
     for side, where in (
-        ("zm", (slice(None), z_first)),
-        ("zp", (slice(None), z_last)),
-        ("ym", (slice(None), slice(None), y_first)),
-        ("yp", (slice(None), slice(None), y_last)),
+        ("zm", (z_first,)),
+        ("zp", (z_last,)),
+        ("ym", (slice(None), y_first)),
+        ("yp", (slice(None), y_last)),
     ):
 
         @pl.when(jnp.logical_not(has[side]))
         def _(side=side, where=where):
-            shape = ext_k[where].shape
-            ext_k[where] = jnp.full(shape, DEAD, BF16)
-            ext_v[where] = jnp.zeros(shape, BF16)
+            shape = ext[(slice(None), 0) + where].shape
+            ext[(slice(None), 0) + where] = jnp.full(shape, DEAD, BF16)
+            ext[(slice(None), 1) + where] = jnp.zeros(shape, BF16)
             got = got_z if side[0] == "z" else got_y
             slot = 0 if side[1] == "m" else 1
             got[:, slot] = jnp.zeros(got[:, slot].shape, BF16)
@@ -281,24 +308,24 @@
     for o in range(27):
         filt[o] = jnp.broadcast_to(w_ref[o : o + 1].astype(F32), filt.shape[1:])
 
-    def own_row(y, carry):
+    def own_row(y):
         for g in range(groups):
             part = parts[g]
             for z in range(depth):
                 q_row = q_ref[z, y, :, part].astype(F32)
                 g_row = g_ref[z, y, :, part].astype(F32)
                 for h in range(GROUP_HEADS):
-                    at = pl.ds((z * GROUP_HEADS + h) * cols, cols)
+                    at = pl.ds(((y % 2) * depth * GROUP_HEADS + z * GROUP_HEADS + h) * cols, cols)
                     mine = lane_head == h
-                    qm[g, y, at] = jnp.where(mine, q_row, 0.0).astype(BF16)
-                    gm[g, y, at] = jnp.where(mine, g_row, 0.0).astype(BF16)
+                    qm[g, y // 2, at] = jnp.where(mine, q_row, 0.0).astype(BF16)
+                    gm[g, y // 2, at] = jnp.where(mine, g_row, 0.0).astype(BF16)
                 none = jnp.zeros((1, LANES), F32)
                 shifted[g, 0, z, y] = jnp.concatenate([g_row[1:], none], axis=0)
                 shifted[g, 1, z, y] = g_row
                 shifted[g, 2, z, y] = jnp.concatenate([none, g_row[:-1]], axis=0)
-        return carry
-
-    lax.fori_loop(0, rows, own_row, 0)
+
+    for y in range(rows):
+        own_row(y)
     acc[...] = jnp.zeros(acc.shape, F32)
     eights[27:] = jnp.zeros((5, 8, eights.shape[2]), F32)
     octets = (depth * rows * cols // 8, 8, LANES)
@@ -323,43 +350,50 @@
                 if not own <= z <= own + 4:
                     reach = jnp.logical_and(reach, half != own)
             live = jnp.where(reach, 1.0, 0.0)
-            mask[z] = jnp.where(ext_k[0, z].astype(F32) < 3.0, live, 0.0)
+            mask[z] = jnp.where(ext[0, 0, z].astype(F32) < 3.0, live, 0.0)
 
     scaling = HEAD**-0.5
-    keys_n = (depth + 4) * 5 * cols
-    head_row = lax.broadcasted_iota(jnp.int32, (depth * GROUP_HEADS * cols, LANES), 0)
+    keys_n = (depth + 4) * 6 * cols
+    head_row = lax.broadcasted_iota(jnp.int32, (2 * depth * GROUP_HEADS * cols, LANES), 0)
     head_row = (head_row // cols) % GROUP_HEADS
     own_head = head_row == lax.broadcasted_iota(jnp.int32, head_row.shape, 1) // HEAD
-
-    def attend(g):
-        def row(y, carry):
-            near = pl.ds(y, 5)
-            keys = ext_k[g, :, near].reshape(keys_n, LANES)
-            values = ext_v[g, :, near].reshape(keys_n, LANES)
-            queries, grads = qm[g, y], gm[g, y]
-            nt = (((1,), (1,)), ((), ()))
-            tn = (((0,), (0,)), ((), ()))
-            scores = lax.dot_general(keys, queries, nt, preferred_element_type=F32)
-            weights = jnp.exp2(scores * (scaling * LOG2E)) * mask[:, near].reshape(keys_n, LANES)
-            totals = jnp.sum(weights, axis=0, keepdims=True) + (1.0 - lane_keep)
+    nt = (((1,), (1,)), ((), ()))
+    tn = (((0,), (0,)), ((), ()))
+
+    def beside(first, second):
+        none = jnp.zeros((depth + 4, 1, cols, LANES), first.dtype)
+        first = jnp.concatenate([first, none], axis=1)
+        second = jnp.concatenate([none, second], axis=1)
+        return jnp.concatenate([first, second], axis=-1).reshape(keys_n, 2 * LANES)
+
+    def attend(g, pair):
+        y = 2 * pair
+        keys = ext[g, 0, :, y : y + 6].reshape(keys_n, LANES)
+        values = ext[g, 1, :, y : y + 6].reshape(keys_n, LANES)
+        queries, grads = qm[g, pair], gm[g, pair]
+        shape = (depth + 4, 6, cols, 2 * LANES)
+        scores = lax.dot_general(keys, queries, nt, preferred_element_type=F32).reshape(shape)
+        dprobs = lax.dot_general(values, grads, nt, preferred_element_type=F32).reshape(shape)
+        lows, dscores = [], []
+        for i in range(2):
+            part = slice(i * LANES, (i + 1) * LANES)
+            weights = jnp.exp2(scores[:, i : i + 5, :, part] * (scaling * LOG2E)) * mask[:, y + i : y + i + 5]
+            totals = jnp.sum(weights, axis=(0, 1, 2), keepdims=True) + (1.0 - lane_keep)
             probs = weights * (lane_keep / totals)
-            probs_low = probs.astype(BF16)
-            dprobs = lax.dot_general(values, grads, nt, preferred_element_type=F32)
-            deltas = jnp.sum(probs_low.astype(F32) * dprobs, axis=0, keepdims=True)
-            dscores = (scaling * probs * (dprobs - deltas)).astype(BF16)
-            shape = (depth + 4, 5, cols, LANES)
-            acc[g, 1, :, near] += jnp.dot(
-                probs_low, grads, preferred_element_type=F32
-            ).reshape(shape)
-            acc[g, 0, :, near] += jnp.dot(
-                dscores, queries, preferred_element_type=F32
-            ).reshape(shape)
-            dq = lax.dot_general(dscores, keys, tn, preferred_element_type=F32)
-            dq = jnp.where(own_head, dq, 0.0).reshape(depth, GROUP_HEADS, cols, LANES)
-            gq_ref[:, pl.ds(y, 1), :, parts[g]] = jnp.sum(dq, axis=1)[:, None].astype(BF16)
-            return carry
-
-        return row
+            low = probs.astype(BF16)
+            dprob = dprobs[:, i : i + 5, :, part]
+            deltas = jnp.sum(low.astype(F32) * dprob, axis=(0, 1, 2), keepdims=True)
+            lows.append(low)
+            dscores.append((scaling * probs * (dprob - deltas)).astype(BF16))
+        low, dscore = beside(*lows), beside(*dscores)
+        shape = (depth + 4, 6, cols, LANES)
+        acc[g, 1, :, y : y + 6] += jnp.dot(low, grads, preferred_element_type=F32).reshape(shape)
+        acc[g, 0, :, y : y + 6] += jnp.dot(dscore, queries, preferred_element_type=F32).reshape(shape)
+        dq = lax.dot_general(dscore, keys, tn, preferred_element_type=F32)
+        dq = jnp.where(own_head, dq, 0.0).reshape(2, depth, GROUP_HEADS, cols, LANES)
+        dq = jnp.sum(dq, axis=2).astype(BF16)
+        for i in range(2):
+            gq_ref[:, y + i, :, parts[g]] = dq[i]
 
     def part_copy(g, stage, slot):
         if stage == "y":
@@ -423,11 +457,12 @@
             out[:, :, :, parts[g]] = total.astype(BF16)
 
     def filter_terms():
-        near_v[:, 1 : 1 + depth, 1 : 1 + rows] = ext_v[:, 2 : 2 + depth, 2 : 2 + rows]
-        near_v[:, 0, 1 : 1 + rows] = ext_v[:, 1, 2 : 2 + rows]
-        near_v[:, 1 + depth, 1 : 1 + rows] = ext_v[:, 2 + depth, 2 : 2 + rows]
-        near_v[:, 1 : 1 + depth, 0] = ext_v[:, 2 : 2 + depth, 1]
-        near_v[:, 1 : 1 + depth, 1 + rows] = ext_v[:, 2 : 2 + depth, 2 + rows]
+        values = ext.at[:, 1]
+        near_v[:, 1 : 1 + depth, 1 : 1 + rows] = values[:, 2 : 2 + depth, 2 : 2 + rows]
+        near_v[:, 0, 1 : 1 + rows] = values[:, 1, 2 : 2 + rows]
+        near_v[:, 1 + depth, 1 : 1 + rows] = values[:, 2 + depth, 2 : 2 + rows]
+        near_v[:, 1 : 1 + depth, 0] = values[:, 2 : 2 + depth, 1]
+        near_v[:, 1 : 1 + depth, 1 + rows] = values[:, 2 : 2 + depth, 2 + rows]
 
         def one(i, carry):
             oz, oy = lax.div(i, 3), lax.rem(i, 3)
@@ -457,7 +492,7 @@
             halves[g] = total[:, parts[g]]
         half_copy(0).start()
 
-    def sum_copy(r, step):
+    def sum_copy(r, moves):
         digits = sum_rounds[r]
         me = member_of(digits)
         return pltpu.make_async_remote_copy(
@@ -465,7 +500,7 @@
             dst_ref=terms.at[r, me],
             send_sem=sum_send.at[r],
             recv_sem=sum_recv.at[r],
-            device_id=peer(digits, lax.rem(me + step, size_of(digits))),
+            device_id=peer(digits, moves),
             device_id_type=MESH,
         )
 
@@ -482,8 +517,8 @@
 
     def sum_start(r, total):
         terms[r, member_of(sum_rounds[r])] = total.astype(BF16)
-        for step in range(1, size_of(sum_rounds[r])):
-            sum_copy(r, step).start()
+        for moves in moves_of(sum_rounds[r]):
+            sum_copy(r, moves).start()
 
     def sum_first():
         half_copy(0).wait_recv()
@@ -511,45 +546,44 @@
         cg_ref[:, parts[0]] = jnp.where(core == 0, mine, other)
         cg_ref[:, parts[1]] = jnp.where(core == 0, other, mine)
 
-    z_slots, y_slots, m_relays, p_relays = (0, 1), (2, 3), (4, 5), (6, 7)
-
-    def relay(kind):
-        halo_got(kind, z_slots[:1])
-        halo_start(kind, m_relays)
-        halo_got(kind, z_slots[1:])
-        halo_start(kind, p_relays)
+    def relay(g):
+        for source in ("zm", "zp"):
+            halo_got(("v" + str(g), source), ("k" + str(g), source))
+            halo_start(("c", g, "ym", source), ("c", g, "yp", source))
+
+    def arrived(g):
+        halo_got(("ky" + str(g), "ym"), ("ky" + str(g), "yp"))
+        for source in ("zm", "zp"):
+            halo_got(("c", g, "ym", source), ("c", g, "yp", source))
 
     lax.fori_loop(0, 9, filter_values, 0)
-    relay(0)
-    halo_got(0, y_slots)
+    halo_got(("near", "zm"), ("near", "zp"), ("vy", "ym"), ("vy", "yp"))
     for corner in range(4):
 
         @pl.when(both(CORNERS[corner]))
         def _(corner=corner):
             near_copy(corner).wait_recv()
 
+    relay(0)
     filter_terms()
     sum_begin()
     relay(1)
     sum_first()
-    relay(2)
-    halo_got(0, m_relays + p_relays)
-    halo_got(1, y_slots + m_relays + p_relays)
+    arrived(0)
     make_mask()
-    lax.fori_loop(0, 2, attend(0), 0)
+    attend(0, 0)
     send_rows(0, 1)
-    lax.fori_loop(2, rows, attend(0), 0)
+    attend(0, 1)
     send_rows(0, 0)
-    halo_got(2, y_slots + m_relays + p_relays)
-    lax.fori_loop(0, 2, attend(1), 0)
+    arrived(1)
+    attend(1, 0)
     send_rows(1, 1)
-    lax.fori_loop(2, rows, attend(1), 0)
+    attend(1, 1)
     send_rows(1, 0)
+    send_sections(0)
     sum_second()
-    send_sections(0)
     send_sections(1)
-    for kind in range(3):
-        halo_sent(kind, range(8))
+    halo_sent()
     for corner in range(4):
 
         @pl.when(both(opposite(corner)))
@@ -557,10 +591,10 @@
             near_copy(corner).wait_send()
 
     sum_all(0).wait_send()
-    sum_third()
     for g in range(groups):
         for slot in range(2):
             part_sent(g, "y", slot)
+    sum_third()
     finish(0)
     sum_last()
     finish(1)
@@ -591,7 +625,6 @@
     vmem = pl.BlockSpec(memory_space=pltpu.VMEM)
     hbm = pl.BlockSpec(memory_space=pltpu.HBM)
     dma = pltpu.SemaphoreType.DMA
-    ext = (groups, depth + 4, rows + 4, cols, LANES)
     results = pl.pallas_call(
         partial(kernel, sections, rows_n, depth, rows, cols),
         out_shape=(big, big, big, small),
@@ -602,12 +635,11 @@
             pltpu.VMEM(queries.shape, BF16),
             pltpu.VMEM(conv_weight.shape, BF16),
             pltpu.SMEM(block_keep.shape, jnp.int32),
-            pltpu.VMEM(ext, BF16),
-            pltpu.VMEM(ext, BF16),
+            pltpu.VMEM((groups, 2, depth + 4, rows + 4, cols, LANES), BF16),
             pltpu.VMEM((groups, depth + 2, rows + 2, cols, LANES), BF16),
             pltpu.VMEM((groups, 2, depth + 4, rows + 4, cols, LANES), F32),
-            pltpu.VMEM((groups, rows, heads_rows, LANES), BF16),
-            pltpu.VMEM((groups, rows, heads_rows, LANES), BF16),
+            pltpu.VMEM((groups, rows // 2, 2 * heads_rows, LANES), BF16),
+            pltpu.VMEM((groups, rows // 2, 2 * heads_rows, LANES), BF16),
             pltpu.VMEM((groups, 3, depth, rows, cols, LANES), F32),
             pltpu.VMEM((27, 8, channels), F32),
             pltpu.VMEM((32, 8, channels), F32),
@@ -619,8 +651,8 @@
             pltpu.VMEM((4, 32, LANES), F32),
             pltpu.VMEM((2, most, 32, LANES), BF16),
             dma((8,)),
-            dma((3, 8)),
-            dma((3, 8)),
+            dma((HALO_COPIES,)),
+            dma((HALO_COPIES,)),
             dma((4,)),
             dma((4,)),
             dma((groups, 2)),

time: 38.6 us -> 36.6 us (0.948)
  the two profiles are of different devices: /device:TPU:31 before, /device:TPU:65 now
where the time goes in v3:
time: 36.6 us; the launch traced here: 36.5 us
  Pallas kernels  35.8 us (98%)
  between operations  0.64 us (2%)
    pallas_call x1, Pallas kernels, shards(): pl.pallas_call(partial(kernel, sections, rows_n, depth, rows, cols), out_...  34.2 us
    pallas_call x1, Pallas kernels, shards(): pl.pallas_call(write_out, out_shape=(big, big, big, small), in_specs=[vme...  1.62 us

profile of v3, /device:TPU:65, one launch (start us, length us, event | category | flops | bytes accessed | tf_op | source)
XLA Modules:
  0.0 36.5 jit_solution(13509678594846851371)
XLA Ops:
  0.6 34.2 %shard_map.93 = (bf16[2,4,16,256]{3,2,1,0:T(8,128)(2,1)}, bf16[2,4,16,256]{3,2,1,0:T(8,128)(2,1)}, bf16[2,4,16,256]{3,2,1,0:T(8,128)(2,1)}, f32[27,256]{1,0:T(8,128)}) custom-call(bf16[2,4,16,256]{3,2,1,0:T(8,128)(2,1)} %q_hbm.1, bf16[2,4,16,256]{3,2,1,0:T(8,128)(2,1)} %k_hbm.1, bf16[2,4,16,256]{3,2,1,0:T(8,128)(2,1)} %v_hbm.1, ...), custom_call_target="tpu_custom_call" | custom-call | tf_op jit(solution)/shard_map/pallas_call | solution.py:628
  34.8 1.6 %shard_map.94 = (bf16[2,4,16,256]{3,2,1,0:T(8,128)(2,1)}, bf16[2,4,16,256]{3,2,1,0:T(8,128)(2,1)}, bf16[2,4,16,256]{3,2,1,0:T(8,128)(2,1)}, f32[27,256]{1,0:T(8,128)}) custom-call(bf16[2,4,16,256]{3,2,1,0:T(8,128)(2,1)} %get-tuple-element.8.refs_0_, bf16[2,4,16,256]{3,2,1,0:T(8,128)(2,1)} %get-tuple-element.9.refs_1_, ...), custom_call_target="tpu_custom_call" | custom-call | tf_op jit(solution)/shard_map/pallas_call | solution.py:671

commit v4 on v3

--- a/solution.py
+++ b/solution.py
@@ -89,24 +89,38 @@
     shift = {"zm": -1, "zp": 1, "ym": -1, "yp": 1}
     core = lax.rem(gy, 2)
     partner = (gz, gy + 1 - 2 * core)
+    has["off"] = jnp.logical_or(jnp.logical_and(core == 0, has["ym"]), jnp.logical_and(core == 1, has["yp"]))
     sum_rounds = rounds_of(sections, rows_n)
 
     def both(names):
-        found = has[names[0]]
-        for name in names[1:]:
-            found = jnp.logical_and(found, has[name])
+        found = True
+        for name in names:
+            if name != "on":
+                found = has[name] if found is True else jnp.logical_and(found, has[name])
         return found
 
+    def when(names):
+        found = both(names)
+        return (lambda body: body()) if found is True else pl.when(found)
+
     def device(names):
+        if names == ("on",):
+            return partner
+        if names == ("off",):
+            return (gz, gy - 1 + 2 * core)
         to = dict(place)
         for name in names:
             axis = "g" + name[0]
             to[axis] = to[axis] + shift[name]
         return (to["gz"], to["gy"])
 
+    held = {}
+
     def digit(spec):
-        axis, stride, count = spec
-        return lax.rem(lax.div(place[axis], stride), count)
+        if spec not in held:
+            axis, stride, count = spec
+            held[spec] = lax.rem(lax.div(place[axis], stride), count)
+        return held[spec]
 
     def member_of(digits):
         m = 0
@@ -147,7 +161,7 @@
     loads += [load(v_hbm.at[:, :, :, parts[g]], ext.at[g, 1, z_own, inner], 1 + g) for g in range(groups)]
     loads += [load(k_hbm.at[:, :, :, parts[g]], ext.at[g, 0, z_own, inner], 3 + g) for g in range(groups)]
     loads += [load(g_hbm, g_ref, 5), load(q_hbm, q_ref, 6), load(w_hbm, w_ref, 7)]
-    for copy in loads:
+    for copy in loads[:3]:
         copy.start()
 
     barrier = pltpu.get_barrier_semaphore()
@@ -159,12 +173,12 @@
             pl.semaphore_signal(barrier, inc=1, device_id=device(names), device_id_type=MESH)
 
         expected = expected + both(names).astype(jnp.int32)
-    pl.semaphore_signal(barrier, inc=1, device_id=partner, device_id_type=MESH)
-    expected = expected + 1
     for digits in sum_rounds:
         for moves in moves_of(digits):
             pl.semaphore_signal(barrier, inc=1, device_id=peer(digits, moves), device_id_type=MESH)
         expected = expected + (size_of(digits) - 1)
+    for copy in loads[3:]:
+        copy.start()
 
     loads[0].wait()
     keep_low = keep_ref[0, 0, 0].astype(F32)
@@ -193,32 +207,34 @@
             return (g, 1, pl.ds(behind[to], 1), inner), (g, 1, pl.ds(behind[to] + far[to], 1), inner)
         return (g, 0, z_own, inner), (g, 0, z_first if to == "zp" else z_last, inner)
 
+    sides = {
+        "on": (pl.ds(rows - 2 * core, 2), pl.ds((2 + rows) * core, 2), pl.ds((2 + rows) * (1 - core), 2)),
+        "off": (pl.ds(2 + 2 * core, 2), pl.ds((2 + rows) * (1 - core), 2), pl.ds((2 + rows) * core, 2)),
+    }
     halo = []
     index = {}
     for name in ["near"] + [kind + str(g) for g in range(groups) for kind in ("v", "k")]:
         for to, source in (("zp", "zm"), ("zm", "zp")):
             src, dst = along_z(name, to)
             index[name, source] = len(halo)
-            halo.append(((to,), src, dst, (source,)))
-    for name, at in [("vy", (every, 1))] + [("ky" + str(g), (g, 0)) for g in range(groups)]:
-        index[name, "ym"] = len(halo)
-        halo.append((("yp",), at + (z_own, high), at + (z_own, y_first), ("ym",)))
-        index[name, "yp"] = len(halo)
-        halo.append((("ym",), at + (z_own, low), at + (z_own, y_last), ("yp",)))
-    for g in range(groups):
-        kv = pl.ds(0, 2)
-        for source, z in (("zm", z_first), ("zp", z_last)):
-            index["c", g, "ym", source] = len(halo)
-            halo.append((("yp", source), (g, kv, z, high), (g, kv, z, y_first), ("ym", source)))
-            index["c", g, "yp", source] = len(halo)
-            halo.append((("ym", source), (g, kv, z, low), (g, kv, z, y_last), ("yp", source)))
+            halo.append(((to,), src, dst, (source,), dst))
+    for side, (sent, there, here) in sides.items():
+        for name, at in [("vy", (every, 1))] + [("ky" + str(g), (g, 0)) for g in range(groups)]:
+            index[name, side] = len(halo)
+            halo.append(((side,), at + (z_own, sent), at + (z_own, there), (side,), at + (z_own, here)))
+        for g in range(groups):
+            at = (g, pl.ds(0, 2))
+            for source, z in (("zm", z_first), ("zp", z_last)):
+                index["c", g, side, source] = len(halo)
+                names = (side, source)
+                halo.append((names, at + (z, sent), at + (z, there), names, at + (z, here)))
     assert len(halo) == HALO_COPIES
 
-    def halo_copy(slot):
-        to, src, dst, _ = halo[slot]
+    def halo_copy(slot, here=False):
+        to, src, dst, _, dst_here = halo[slot]
         return pltpu.make_async_remote_copy(
             src_ref=ext.at[src],
-            dst_ref=ext.at[dst],
+            dst_ref=ext.at[dst_here if here else dst],
             send_sem=halo_send.at[slot],
             recv_sem=halo_recv.at[slot],
             device_id=device(to[:1]),
@@ -229,7 +245,7 @@
         for name in names:
             slot = index[name]
 
-            @pl.when(both(halo[slot][0]))
+            @when(halo[slot][0])
             def _(slot=slot):
                 halo_copy(slot).start()
 
@@ -237,14 +253,14 @@
         for name in names:
             slot = index[name]
 
-            @pl.when(both(halo[slot][3]))
+            @when(halo[slot][3])
             def _(slot=slot):
-                halo_copy(slot).wait_recv()
+                halo_copy(slot, here=True).wait_recv()
 
     def halo_sent():
         for slot in range(len(halo)):
 
-            @pl.when(both(halo[slot][0]))
+            @when(halo[slot][0])
             def _(slot=slot):
                 halo_copy(slot).wait_send()
 
@@ -262,7 +278,7 @@
     def opposite(corner):
         return tuple(name[0] + ("p" if name[1] == "m" else "m") for name in CORNERS[corner])
 
-    halo_start(("near", "zm"), ("near", "zp"), ("vy", "ym"), ("vy", "yp"))
+    halo_start(("near", "zm"), ("near", "zp"), ("vy", "off"), ("vy", "on"))
     for corner in range(4):
 
         @pl.when(both(opposite(corner)))
@@ -277,7 +293,7 @@
     for g in range(groups):
         for kind in ("v", "k"):
             halo_start((kind + str(g), "zm"), (kind + str(g), "zp"))
-        halo_start(("ky" + str(g), "ym"), ("ky" + str(g), "yp"))
+        halo_start(("ky" + str(g), "off"), ("ky" + str(g), "on"))
 
     for side, where in (
         ("zm", (z_first,)),
@@ -343,14 +359,14 @@
     band = jnp.abs(row_x - lane_x) <= 2
     half = lax.broadcasted_iota(jnp.int32, (cols, LANES), 1) // (GROUP_HEADS * cols)
 
-    def make_mask():
+    def make_mask(near):
         for z in range(depth + 4):
             reach = band
             for own in range(depth):
                 if not own <= z <= own + 4:
                     reach = jnp.logical_and(reach, half != own)
             live = jnp.where(reach, 1.0, 0.0)
-            mask[z] = jnp.where(ext[0, 0, z].astype(F32) < 3.0, live, 0.0)
+            mask[z, near] = jnp.where(ext[0, 0, z, near].astype(F32) < 3.0, live, 0.0)
 
     scaling = HEAD**-0.5
     keys_n = (depth + 4) * 6 * cols
@@ -368,8 +384,8 @@
 
     def attend(g, pair):
         y = 2 * pair
-        keys = ext[g, 0, :, y : y + 6].reshape(keys_n, LANES)
-        values = ext[g, 1, :, y : y + 6].reshape(keys_n, LANES)
+        keys = ext[g, 0, :, pl.ds(y, 6)].reshape(keys_n, LANES)
+        values = ext[g, 1, :, pl.ds(y, 6)].reshape(keys_n, LANES)
         queries, grads = qm[g, pair], gm[g, pair]
         shape = (depth + 4, 6, cols, 2 * LANES)
         scores = lax.dot_general(keys, queries, nt, preferred_element_type=F32).reshape(shape)
@@ -377,7 +393,7 @@
         lows, dscores = [], []
         for i in range(2):
             part = slice(i * LANES, (i + 1) * LANES)
-            weights = jnp.exp2(scores[:, i : i + 5, :, part] * (scaling * LOG2E)) * mask[:, y + i : y + i + 5]
+            weights = jnp.exp2(scores[:, i : i + 5, :, part] * (scaling * LOG2E)) * mask[:, pl.ds(y + i, 5)]
             totals = jnp.sum(weights, axis=(0, 1, 2), keepdims=True) + (1.0 - lane_keep)
             probs = weights * (lane_keep / totals)
             low = probs.astype(BF16)
@@ -387,74 +403,103 @@
             dscores.append((scaling * probs * (dprob - deltas)).astype(BF16))
         low, dscore = beside(*lows), beside(*dscores)
         shape = (depth + 4, 6, cols, LANES)
-        acc[g, 1, :, y : y + 6] += jnp.dot(low, grads, preferred_element_type=F32).reshape(shape)
-        acc[g, 0, :, y : y + 6] += jnp.dot(dscore, queries, preferred_element_type=F32).reshape(shape)
-        dq = lax.dot_general(dscore, keys, tn, preferred_element_type=F32)
-        dq = jnp.where(own_head, dq, 0.0).reshape(2, depth, GROUP_HEADS, cols, LANES)
-        dq = jnp.sum(dq, axis=2).astype(BF16)
-        for i in range(2):
-            gq_ref[:, y + i, :, parts[g]] = dq[i]
-
-    def part_copy(g, stage, slot):
-        if stage == "y":
-            src, dst, sends, recvs = part_y, got_y, py_send, py_recv
-        else:
-            src, dst, sends, recvs = part_z, got_z, pz_send, pz_recv
-        to = stage + ("p" if slot == 0 else "m")
-        source = stage + ("m" if slot == 0 else "p")
-        copy = pltpu.make_async_remote_copy(
-            src_ref=src.at[g, slot],
-            dst_ref=dst.at[g, slot],
-            send_sem=sends.at[g, slot],
-            recv_sem=recvs.at[g, slot],
-            device_id=device((to,)),
+        acc[g, 1, :, pl.ds(y, 6)] += jnp.dot(low, grads, preferred_element_type=F32).reshape(shape)
+        acc[g, 0, :, pl.ds(y, 6)] += jnp.dot(dscore, queries, preferred_element_type=F32).reshape(shape)
+
+        def own_queries():
+            dq = lax.dot_general(dscore, keys, tn, preferred_element_type=F32)
+            dq = jnp.where(own_head, dq, 0.0).reshape(2, depth, GROUP_HEADS, cols, LANES)
+            dq = jnp.sum(dq, axis=2).astype(BF16)
+            for i in range(2):
+                gq_ref[:, pl.ds(y + i, 1), :, parts[g]] = dq[i][:, None]
+
+        return own_queries
+
+    first, later = pl.ds(0, 4), pl.ds(4, depth)
+
+    def rows_copy(g, side, stage, here=False):
+        slot = core if (side == "on") != here else 1 - core
+        z = later if stage else first
+        return pltpu.make_async_remote_copy(
+            src_ref=part_y.at[g, slot, :, z],
+            dst_ref=got_y.at[g, slot, :, z],
+            send_sem=py_send.at[g, slot, stage],
+            recv_sem=py_recv.at[g, slot, stage],
+            device_id=device((side,)),
             device_id_type=MESH,
         )
-        return to, source, copy
-
-    def part_start(g, stage, slot):
-        to, _, copy = part_copy(g, stage, slot)
-
-        @pl.when(has[to])
+
+    def send_rows(g, side):
+        slot = core if side == "on" else 1 - core
+        at = pl.ds((2 + rows) * (1 - slot), 2)
+        part_y[g, slot, :, 0:2] = acc[g, :, 0:2, at].astype(BF16)
+        part_y[g, slot, :, 2:4] = acc[g, :, 2 + depth : 4 + depth, at].astype(BF16)
+        part_y[g, slot, :, 4 : 4 + depth] = acc[g, :, 2 : 2 + depth, at].astype(BF16)
+
+        @when((side,))
         def _():
-            copy.start()
-
-    def part_got(g, stage, slot):
-        _, source, copy = part_copy(g, stage, slot)
-
-        @pl.when(has[source])
+            rows_copy(g, side, 0).start()
+            rows_copy(g, side, 1).start()
+
+    def got_rows(g, side, stage):
+        @when((side,))
         def _():
-            copy.wait_recv()
-
-    def part_sent(g, stage, slot):
-        to, _, copy = part_copy(g, stage, slot)
-
-        @pl.when(has[to])
-        def _():
-            copy.wait_send()
-
-    def send_rows(g, slot):
-        at = 2 + rows if slot == 0 else 0
-        part_y[g, slot] = acc[g, :, :, at : at + 2].astype(BF16)
-        part_start(g, "y", slot)
-
-    def send_sections(g):
-        part_got(g, "y", 0)
-        part_got(g, "y", 1)
-        acc[g, :, :, 2:4] += got_y[g, 0].astype(F32)
-        acc[g, :, :, rows : rows + 2] += got_y[g, 1].astype(F32)
-        for slot in range(2):
-            at = 2 + depth if slot == 0 else 0
-            part_z[g, slot] = acc[g, :, at : at + 2, 2 : 2 + rows].astype(BF16)
-            part_start(g, "z", slot)
+            rows_copy(g, side, stage, here=True).wait_recv()
+
+    def sections_copy(g, place_, slot):
+        return pltpu.make_async_remote_copy(
+            src_ref=part_z.at[g, place_, slot],
+            dst_ref=got_z.at[g, place_, slot],
+            send_sem=pz_send.at[g, place_, slot],
+            recv_sem=pz_recv.at[g, place_, slot],
+            device_id=device(("zp" if place_ == 0 else "zm",)),
+            device_id_type=MESH,
+        )
+
+    def send_sections(g, side):
+        slot = 1 - core if side == "on" else core
+        got_rows(g, side, 0)
+        near = pl.ds(2 + 2 * slot, 2)
+        for place_, z in ((0, 2 + depth), (1, 0)):
+            given = got_y[g, slot, :, 2 * (1 - place_) : 2 * (2 - place_)].astype(F32)
+            part_z[g, place_, slot] = (acc[g, :, z : z + 2, near] + given).astype(BF16)
+
+            @pl.when(has["zp" if place_ == 0 else "zm"])
+            def _(place_=place_):
+                sections_copy(g, place_, slot).start()
 
     def finish(g):
-        part_got(g, "z", 0)
-        part_got(g, "z", 1)
+        got_rows(g, "on", 1)
+        got_rows(g, "off", 1)
+        for place_, source in ((0, "zm"), (1, "zp")):
+
+            @pl.when(has[source])
+            def _(place_=place_):
+                for slot in range(2):
+                    sections_copy(g, place_, slot).wait_recv()
+
         for kind, out in ((0, gk_ref), (1, gv_ref)):
-            total = acc[g, kind, 2 : 2 + depth, 2 : 2 + rows]
-            total = total + got_z[g, 0, kind].astype(F32) + got_z[g, 1, kind].astype(F32)
-            out[:, :, :, parts[g]] = total.astype(BF16)
+            for slot in range(2):
+                near = slice(2 + 2 * slot, 4 + 2 * slot)
+                total = acc[g, kind, 2 : 2 + depth, near] + got_y[g, slot, kind, 4 : 4 + depth].astype(F32)
+                total = total + got_z[g, 0, slot, kind].astype(F32) + got_z[g, 1, slot, kind].astype(F32)
+                out[:, 2 * slot : 2 * slot + 2, :, parts[g]] = total.astype(BF16)
+
+    def rows_sent(g):
+        for side in ("on", "off"):
+
+            @when((side,))
+            def _(side=side):
+                rows_copy(g, side, 0).wait_send()
+                rows_copy(g, side, 1).wait_send()
+
+    def sections_sent(g):
+        for place_, to in ((0, "zp"), (1, "zm")):
+
+            @pl.when(has[to])
+            def _(place_=place_):
+                for slot in range(2):
+                    sections_copy(g, place_, slot).wait_send()
 
     def filter_terms():
         values = ext.at[:, 1]
@@ -549,40 +594,47 @@
     def relay(g):
         for source in ("zm", "zp"):
             halo_got(("v" + str(g), source), ("k" + str(g), source))
-            halo_start(("c", g, "ym", source), ("c", g, "yp", source))
-
-    def arrived(g):
-        halo_got(("ky" + str(g), "ym"), ("ky" + str(g), "yp"))
-        for source in ("zm", "zp"):
-            halo_got(("c", g, "ym", source), ("c", g, "yp", source))
+            halo_start(("c", g, "off", source), ("c", g, "on", source))
+
+    def arrived(g, side):
+        halo_got(("ky" + str(g), side), ("c", g, side, "zm"), ("c", g, side, "zp"))
 
     lax.fori_loop(0, 9, filter_values, 0)
-    halo_got(("near", "zm"), ("near", "zp"), ("vy", "ym"), ("vy", "yp"))
+    halo_got(("near", "zm"), ("near", "zp"), ("vy", "on"), ("vy", "off"))
     for corner in range(4):
 
         @pl.when(both(CORNERS[corner]))
         def _(corner=corner):
             near_copy(corner).wait_recv()
 
-    relay(0)
     filter_terms()
     sum_begin()
+    relay(0)
+    sum_first()
     relay(1)
-    sum_first()
-    arrived(0)
-    make_mask()
-    attend(0, 0)
-    send_rows(0, 1)
-    attend(0, 1)
-    send_rows(0, 0)
-    arrived(1)
-    attend(1, 0)
-    send_rows(1, 1)
-    attend(1, 1)
-    send_rows(1, 0)
-    send_sections(0)
+    arrived(0, "on")
+    make_mask(pl.ds(2 * (1 - core), 6))
+    own_queries = attend(0, 1 - core)
+    send_rows(0, "on")
+    own_queries()
+    arrived(0, "off")
+    make_mask(pl.ds((2 + rows) * core, 2))
+    own_queries = attend(0, core)
+    send_rows(0, "off")
+    own_queries()
+    arrived(1, "on")
+    own_queries = attend(1, 1 - core)
+    send_rows(1, "on")
+    own_queries()
+    send_sections(0, "on")
+    arrived(1, "off")
+    own_queries = attend(1, core)
+    send_rows(1, "off")
+    own_queries()
+    send_sections(0, "off")
+    send_sections(1, "on")
     sum_second()
-    send_sections(1)
+    send_sections(1, "off")
     halo_sent()
     for corner in range(4):
 
@@ -592,17 +644,15 @@
 
     sum_all(0).wait_send()
     for g in range(groups):
-        for slot in range(2):
-            part_sent(g, "y", slot)
+        rows_sent(g)
     sum_third()
+    sections_sent(0)
+    sum_all(1).wait_send()
     finish(0)
     sum_last()
+    half_copy(1).wait_send()
+    sections_sent(1)
     finish(1)
-    for g in range(groups):
-        for slot in range(2):
-            part_sent(g, "z", slot)
-    sum_all(1).wait_send()
-    half_copy(1).wait_send()
 
 
 def write_out(*refs):
@@ -646,8 +696,8 @@
             pltpu.VMEM((depth + 4, rows + 4, cols, LANES), F32),
             pltpu.VMEM((groups, 2, 2, depth + 4, 2, cols, LANES), BF16),
             pltpu.VMEM((groups, 2, 2, depth + 4, 2, cols, LANES), BF16),
-            pltpu.VMEM((groups, 2, 2, 2, rows, cols, LANES), BF16),
-            pltpu.VMEM((groups, 2, 2, 2, rows, cols, LANES), BF16),
+            pltpu.VMEM((groups, 2, 2, 2, 2, 2, cols, LANES), BF16),
+            pltpu.VMEM((groups, 2, 2, 2, 2, 2, cols, LANES), BF16),
             pltpu.VMEM((4, 32, LANES), F32),
             pltpu.VMEM((2, most, 32, LANES), BF16),
             dma((8,)),
@@ -655,10 +705,10 @@
             dma((HALO_COPIES,)),
             dma((4,)),
             dma((4,)),
-            dma((groups, 2)),
-            dma((groups, 2)),
-            dma((groups, 2)),
-            dma((groups, 2)),
+            dma((groups, 2, 2)),
+            dma((groups, 2, 2)),
+            dma((groups, 2, 2)),
+            dma((groups, 2, 2)),
             dma((2,)),
             dma((2,)),
             dma((2,)),

time: 36.6 us -> 36.1 us (0.986)
  the two profiles are of different devices: /device:TPU:65 before, /device:TPU:31 now
where the time goes in v4:
time: 36.1 us; the launch traced here: 35.9 us
  Pallas kernels  35.3 us (98%)
  between operations  0.64 us (2%)
    pallas_call x1, Pallas kernels, shards(): pl.pallas_call(partial(kernel, sections, rows_n, depth, rows, cols), out_...  33.7 us
    pallas_call x1, Pallas kernels, shards(): pl.pallas_call(write_out, out_shape=(big, big, big, small), in_specs=[vme...  1.62 us

profile of v4, /device:TPU:31, one launch (start us, length us, event | category | flops | bytes accessed | tf_op | source)
XLA Modules:
  0.0 35.9 jit_solution(9043339393278996646)
XLA Ops:
  0.6 33.7 %shard_map.93 = (bf16[2,4,16,256]{3,2,1,0:T(8,128)(2,1)}, bf16[2,4,16,256]{3,2,1,0:T(8,128)(2,1)}, bf16[2,4,16,256]{3,2,1,0:T(8,128)(2,1)}, f32[27,256]{1,0:T(8,128)}) custom-call(bf16[2,4,16,256]{3,2,1,0:T(8,128)(2,1)} %q_hbm.1, bf16[2,4,16,256]{3,2,1,0:T(8,128)(2,1)} %k_hbm.1, bf16[2,4,16,256]{3,2,1,0:T(8,128)(2,1)} %v_hbm.1, ...), custom_call_target="tpu_custom_call" | custom-call | tf_op jit(solution)/shard_map/pallas_call | solution.py:678
  34.3 1.6 %shard_map.94 = (bf16[2,4,16,256]{3,2,1,0:T(8,128)(2,1)}, bf16[2,4,16,256]{3,2,1,0:T(8,128)(2,1)}, bf16[2,4,16,256]{3,2,1,0:T(8,128)(2,1)}, f32[27,256]{1,0:T(8,128)}) custom-call(bf16[2,4,16,256]{3,2,1,0:T(8,128)(2,1)} %get-tuple-element.8.refs_0_, bf16[2,4,16,256]{3,2,1,0:T(8,128)(2,1)} %get-tuple-element.9.refs_1_, ...), custom_call_target="tpu_custom_call" | custom-call | tf_op jit(solution)/shard_map/pallas_call | solution.py:721

commit v5 on v4

--- a/solution.py
+++ b/solution.py
@@ -14,6 +14,8 @@
 DEAD = 4.0
 LOG2E = 1.4426950408889634
 HALO_COPIES = 24
+DIRECT_FIRST = ()
+DIRECT_LAST = (1,)
 MESH = pl.DeviceIdType.MESH
 F32 = jnp.float32
 BF16 = jnp.bfloat16
@@ -60,6 +62,7 @@
     got_y,
     part_z,
     got_z,
+    got_c,
     halves,
     terms,
     load_sem,
@@ -69,6 +72,8 @@
     near_recv,
     py_send,
     py_recv,
+    pc_send,
+    pc_recv,
     pz_send,
     pz_recv,
     half_send,
@@ -104,14 +109,13 @@
         return (lambda body: body()) if found is True else pl.when(found)
 
     def device(names):
-        if names == ("on",):
-            return partner
-        if names == ("off",):
-            return (gz, gy - 1 + 2 * core)
         to = dict(place)
         for name in names:
-            axis = "g" + name[0]
-            to[axis] = to[axis] + shift[name]
+            if name in ("on", "off"):
+                to["gy"] = to["gy"] + (1 - 2 * core if name == "on" else 2 * core - 1)
+            else:
+                axis = "g" + name[0]
+                to[axis] = to[axis] + shift[name]
         return (to["gz"], to["gy"])
 
     held = {}
@@ -217,27 +221,32 @@
         for to, source in (("zp", "zm"), ("zm", "zp")):
             src, dst = along_z(name, to)
             index[name, source] = len(halo)
-            halo.append(((to,), src, dst, (source,), dst))
+            halo.append(((to,), src, dst, (source,), dst, (to,)))
     for side, (sent, there, here) in sides.items():
         for name, at in [("vy", (every, 1))] + [("ky" + str(g), (g, 0)) for g in range(groups)]:
             index[name, side] = len(halo)
-            halo.append(((side,), at + (z_own, sent), at + (z_own, there), (side,), at + (z_own, here)))
+            names = (side,)
+            halo.append((names, at + (z_own, sent), at + (z_own, there), names, at + (z_own, here), names))
         for g in range(groups):
             at = (g, pl.ds(0, 2))
             for source, z in (("zm", z_first), ("zp", z_last)):
                 index["c", g, side, source] = len(halo)
                 names = (side, source)
-                halo.append((names, at + (z, sent), at + (z, there), names, at + (z, here)))
+                if side == "off" and g in DIRECT_FIRST:
+                    to = (side, "zp" if source == "zm" else "zm")
+                    halo.append((to, at + (z_own, sent), at + (z, there), names, at + (z, here), to))
+                else:
+                    halo.append((names, at + (z, sent), at + (z, there), names, at + (z, here), (side,)))
     assert len(halo) == HALO_COPIES
 
     def halo_copy(slot, here=False):
-        to, src, dst, _, dst_here = halo[slot]
+        _, src, dst, _, dst_here, to = halo[slot]
         return pltpu.make_async_remote_copy(
             src_ref=ext.at[src],
             dst_ref=ext.at[dst_here if here else dst],
             send_sem=halo_send.at[slot],
             recv_sem=halo_recv.at[slot],
-            device_id=device(to[:1]),
+            device_id=device(to),
             device_id_type=MESH,
         )
 
@@ -294,6 +303,8 @@
         for kind in ("v", "k"):
             halo_start((kind + str(g), "zm"), (kind + str(g), "zp"))
         halo_start(("ky" + str(g), "off"), ("ky" + str(g), "on"))
+    for g in DIRECT_FIRST:
+        halo_start(("c", g, "off", "zm"), ("c", g, "off", "zp"))
 
     for side, where in (
         ("zm", (z_first,)),
@@ -436,10 +447,29 @@
         part_y[g, slot, :, 2:4] = acc[g, :, 2 + depth : 4 + depth, at].astype(BF16)
         part_y[g, slot, :, 4 : 4 + depth] = acc[g, :, 2 : 2 + depth, at].astype(BF16)
 
+        if side == "off" and g in DIRECT_LAST:
+            for place_, to in ((0, "zp"), (1, "zm")):
+
+                @when((side, to))
+                def _(place_=place_):
+                    corner_copy(g, place_).start()
+
         @when((side,))
         def _():
-            rows_copy(g, side, 0).start()
+            if not (side == "off" and g in DIRECT_LAST):
+                rows_copy(g, side, 0).start()
             rows_copy(g, side, 1).start()
+
+    def corner_copy(g, place_, here=False):
+        slot = core if here else 1 - core
+        return pltpu.make_async_remote_copy(
+            src_ref=part_y.at[g, slot, :, pl.ds(2 * (1 - place_), 2)],
+            dst_ref=got_c.at[DIRECT_LAST.index(g), place_],
+            send_sem=pc_send.at[DIRECT_LAST.index(g), place_],
+            recv_sem=pc_recv.at[DIRECT_LAST.index(g), place_],
+            device_id=device(("off", "zp" if place_ == 0 else "zm")),
+            device_id_type=MESH,
+        )
 
     def got_rows(g, side, stage):
         @when((side,))
@@ -458,11 +488,15 @@
 
     def send_sections(g, side):
         slot = 1 - core if side == "on" else core
-        got_rows(g, side, 0)
+        direct = side == "off" and g in DIRECT_LAST
+        if not direct:
+            got_rows(g, side, 0)
         near = pl.ds(2 + 2 * slot, 2)
         for place_, z in ((0, 2 + depth), (1, 0)):
-            given = got_y[g, slot, :, 2 * (1 - place_) : 2 * (2 - place_)].astype(F32)
-            part_z[g, place_, slot] = (acc[g, :, z : z + 2, near] + given).astype(BF16)
+            given = acc[g, :, z : z + 2, near]
+            if not direct:
+                given = given + got_y[g, slot, :, 2 * (1 - place_) : 2 * (2 - place_)].astype(F32)
+            part_z[g, place_, slot] = given.astype(BF16)
 
             @pl.when(has["zp" if place_ == 0 else "zm"])
             def _(place_=place_):
@@ -471,6 +505,16 @@
     def finish(g):
         got_rows(g, "on", 1)
         got_rows(g, "off", 1)
+        if g in DIRECT_LAST:
+            near = pl.ds(2 + 2 * core, 2)
+            for place_, source in ((0, "zm"), (1, "zp")):
+
+                @when(("off", source))
+                def _(place_=place_):
+                    corner_copy(g, place_, here=True).wait_recv()
+                    given = got_c[DIRECT_LAST.index(g), place_].astype(F32)
+                    acc[g, :, 2 : 2 + depth, near] += given
+
         for place_, source in ((0, "zm"), (1, "zp")):
 
             @pl.when(has[source])
@@ -488,9 +532,18 @@
     def rows_sent(g):
         for side in ("on", "off"):
 
+            direct = side == "off" and g in DIRECT_LAST
+            if direct:
+                for place_, to in ((0, "zp"), (1, "zm")):
+
+                    @when((side, to))
+                    def _(place_=place_):
+                        corner_copy(g, place_).wait_send()
+
             @when((side,))
-            def _(side=side):
-                rows_copy(g, side, 0).wait_send()
+            def _(side=side, direct=direct):
+                if not direct:
+                    rows_copy(g, side, 0).wait_send()
                 rows_copy(g, side, 1).wait_send()
 
     def sections_sent(g):
@@ -594,7 +647,7 @@
     def relay(g):
         for source in ("zm", "zp"):
             halo_got(("v" + str(g), source), ("k" + str(g), source))
-            halo_start(("c", g, "off", source), ("c", g, "on", source))
+            halo_start(*(("c", g, side, source) for side in ("off", "on") if side == "on" or g not in DIRECT_FIRST))
 
     def arrived(g, side):
         halo_got(("ky" + str(g), side), ("c", g, side, "zm"), ("c", g, side, "zp"))
@@ -630,11 +683,11 @@
     arrived(1, "off")
     own_queries = attend(1, core)
     send_rows(1, "off")
+    send_sections(1, "off")
     own_queries()
-    send_sections(0, "off")
     send_sections(1, "on")
     sum_second()
-    send_sections(1, "off")
+    send_sections(0, "off")
     halo_sent()
     for corner in range(4):
 
@@ -698,6 +751,7 @@
             pltpu.VMEM((groups, 2, 2, depth + 4, 2, cols, LANES), BF16),
             pltpu.VMEM((groups, 2, 2, 2, 2, 2, cols, LANES), BF16),
             pltpu.VMEM((groups, 2, 2, 2, 2, 2, cols, LANES), BF16),
+            pltpu.VMEM((groups, 2, 2, depth, 2, cols, LANES), BF16),
             pltpu.VMEM((4, 32, LANES), F32),
             pltpu.VMEM((2, most, 32, LANES), BF16),
             dma((8,)),
@@ -707,6 +761,8 @@
             dma((4,)),
             dma((groups, 2, 2)),
             dma((groups, 2, 2)),
+            dma((groups, 2)),
+            dma((groups, 2)),
             dma((groups, 2, 2)),
             dma((groups, 2, 2)),
             dma((2,)),

time: 36.1 us -> 35.6 us (0.986)
  the two profiles are of different devices: /device:TPU:31 before, /device:TPU:38 now
where the time goes in v5:
time: 35.6 us; the launch traced here: 35.4 us
  Pallas kernels  34.8 us (98%)
  between operations  0.64 us (2%)
    pallas_call x1, Pallas kernels, shards(): pl.pallas_call(partial(kernel, sections, rows_n, depth, rows, cols), out_...  33.2 us
    pallas_call x1, Pallas kernels, shards(): pl.pallas_call(write_out, out_shape=(big, big, big, small), in_specs=[vme...  1.62 us

profile of v5, /device:TPU:38, one launch (start us, length us, event | category | flops | bytes accessed | tf_op | source)
XLA Modules:
  0.0 35.4 jit_solution(1139534715781103669)
XLA Ops:
  0.6 33.2 %shard_map.93 = (bf16[2,4,16,256]{3,2,1,0:T(8,128)(2,1)}, bf16[2,4,16,256]{3,2,1,0:T(8,128)(2,1)}, bf16[2,4,16,256]{3,2,1,0:T(8,128)(2,1)}, f32[27,256]{1,0:T(8,128)}) custom-call(bf16[2,4,16,256]{3,2,1,0:T(8,128)(2,1)} %q_hbm.1, bf16[2,4,16,256]{3,2,1,0:T(8,128)(2,1)} %k_hbm.1, bf16[2,4,16,256]{3,2,1,0:T(8,128)(2,1)} %v_hbm.1, ...), custom_call_target="tpu_custom_call" | custom-call | tf_op jit(solution)/shard_map/pallas_call | solution.py:731
  33.8 1.6 %shard_map.94 = (bf16[2,4,16,256]{3,2,1,0:T(8,128)(2,1)}, bf16[2,4,16,256]{3,2,1,0:T(8,128)(2,1)}, bf16[2,4,16,256]{3,2,1,0:T(8,128)(2,1)}, f32[27,256]{1,0:T(8,128)}) custom-call(bf16[2,4,16,256]{3,2,1,0:T(8,128)(2,1)} %get-tuple-element.8.refs_0_, bf16[2,4,16,256]{3,2,1,0:T(8,128)(2,1)} %get-tuple-element.9.refs_1_, ...), custom_call_target="tpu_custom_call" | custom-call | tf_op jit(solution)/shard_map/pallas_call | solution.py:777

commit v6 on v5

--- a/solution.py
+++ b/solution.py
@@ -682,11 +682,11 @@
     send_sections(0, "on")
     arrived(1, "off")
     own_queries = attend(1, core)
+    send_sections(1, "off")
     send_rows(1, "off")
-    send_sections(1, "off")
-    own_queries()
     send_sections(1, "on")
     sum_second()
+    own_queries()
     send_sections(0, "off")
     halo_sent()
     for corner in range(4):
@@ -728,6 +728,7 @@
     vmem = pl.BlockSpec(memory_space=pltpu.VMEM)
     hbm = pl.BlockSpec(memory_space=pltpu.HBM)
     dma = pltpu.SemaphoreType.DMA
+    arguments = (queries, keys, values, cotangent, conv_weight, block_keep)
     results = pl.pallas_call(
         partial(kernel, sections, rows_n, depth, rows, cols),
         out_shape=(big, big, big, small),
@@ -771,15 +772,16 @@
             dma((2,)),
         ],
         compiler_params=pltpu.CompilerParams(
-            collective_id=0, has_side_effects=True, vmem_limit_bytes=60 * 1024 * 1024
+            collective_id=0, has_side_effects=True, vmem_limit_bytes=16 * 1024 * 1024
         ),
-    )(queries, keys, values, cotangent, conv_weight, block_keep)
+    )(*(pltpu.with_memory_space_constraint(x, pltpu.HBM) for x in arguments))
     return pl.pallas_call(
         write_out,
         out_shape=(big, big, big, small),
         in_specs=[vmem] * 4,
         out_specs=(hbm,) * 4,
         scratch_shapes=[dma((4,))],
+        compiler_params=pltpu.CompilerParams(vmem_limit_bytes=1024 * 1024),
     )(*results)
 
 

time: 35.6 us -> 33.9 us (0.952)
  the two profiles are of different devices: /device:TPU:38 before, /device:TPU:31 now
where the time goes in v6:
time: 33.9 us; the launch traced here: 33.6 us
  Pallas kernels  33 us (97%)
  between operations  0.64 us (2%)
    pallas_call x1, Pallas kernels, shards(): pl.pallas_call(partial(kernel, sections, rows_n, depth, rows, cols), out_...  32.2 us
    pallas_call x1, Pallas kernels, shards(): pl.pallas_call(write_out, out_shape=(big, big, big, small), in_specs=[vme...  0.72 us

profile of v6, /device:TPU:31, one launch (start us, length us, event | category | flops | bytes accessed | tf_op | source)
XLA Modules:
  0.0 33.6 jit_solution(3010372996381375498)
XLA Ops:
  0.6 32.2 %shard_map.93 = (bf16[2,4,16,256]{3,2,1,0:T(8,128)(2,1)S(1)}, bf16[2,4,16,256]{3,2,1,0:T(8,128)(2,1)S(1)}, bf16[2,4,16,256]{3,2,1,0:T(8,128)(2,1)S(1)}, f32[27,256]{1,0:T(8,128)S(1)}) custom-call(bf16[2,4,16,256]{3,2,1,0:T(8,128)(2,1)} %q_hbm.1, bf16[2,4,16,256]{3,2,1,0:T(8,128)(2,1)} %k_hbm.1, bf16[2,4,16,256]{3,2,1,0:T(8,128)(2,1)} %v_hbm.1, ...), custom_call_target="tpu_custom_call" | custom-call | tf_op jit(solution)/shard_map/pallas_call | solution.py:732
  32.9 0.7 %shard_map.94 = (bf16[2,4,16,256]{3,2,1,0:T(8,128)(2,1)}, bf16[2,4,16,256]{3,2,1,0:T(8,128)(2,1)}, bf16[2,4,16,256]{3,2,1,0:T(8,128)(2,1)}, f32[27,256]{1,0:T(8,128)}) custom-call(bf16[2,4,16,256]{3,2,1,0:T(8,128)(2,1)S(1)} %get-tuple-element.8.refs_0_, bf16[2,4,16,256]{3,2,1,0:T(8,128)(2,1)S(1)} %get-tuple-element.9.refs_1_, ...), custom_call_target="tpu_custom_call" | custom-call | tf_op jit(solution)/shard_map/pallas_call | solution.py:778

commit v7 on v6

--- a/solution.py
+++ b/solution.py
@@ -165,7 +165,7 @@
     loads += [load(v_hbm.at[:, :, :, parts[g]], ext.at[g, 1, z_own, inner], 1 + g) for g in range(groups)]
     loads += [load(k_hbm.at[:, :, :, parts[g]], ext.at[g, 0, z_own, inner], 3 + g) for g in range(groups)]
     loads += [load(g_hbm, g_ref, 5), load(q_hbm, q_ref, 6), load(w_hbm, w_ref, 7)]
-    for copy in loads[:3]:
+    for copy in loads[:5]:
         copy.start()
 
     barrier = pltpu.get_barrier_semaphore()
@@ -181,7 +181,7 @@
         for moves in moves_of(digits):
             pl.semaphore_signal(barrier, inc=1, device_id=peer(digits, moves), device_id_type=MESH)
         expected = expected + (size_of(digits) - 1)
-    for copy in loads[3:]:
+    for copy in loads[5:]:
         copy.start()
 
     loads[0].wait()
@@ -688,6 +688,7 @@
     sum_second()
     own_queries()
     send_sections(0, "off")
+    sum_third()
     halo_sent()
     for corner in range(4):
 
@@ -698,7 +699,6 @@
     sum_all(0).wait_send()
     for g in range(groups):
         rows_sent(g)
-    sum_third()
     sections_sent(0)
     sum_all(1).wait_send()
     finish(0)

time: 33.9 us -> 33.9 us (level)
  no operation moved by 1% of the time
where the time goes in v7:
time: 33.9 us; the launch traced here: 33.6 us
  Pallas kernels  33 us (97%)
  between operations  0.64 us (2%)
    pallas_call x1, Pallas kernels, shards(): pl.pallas_call(partial(kernel, sections, rows_n, depth, rows, cols), out_...  32.3 us
    pallas_call x1, Pallas kernels, shards(): pl.pallas_call(write_out, out_shape=(big, big, big, small), in_specs=[vme...  0.72 us

profile of v7, /device:TPU:31, one launch (start us, length us, event | category | flops | bytes accessed | tf_op | source)
XLA Modules:
  0.0 33.6 jit_solution(14370278772096115210)
XLA Ops:
  0.6 32.3 %shard_map.93 = (bf16[2,4,16,256]{3,2,1,0:T(8,128)(2,1)S(1)}, bf16[2,4,16,256]{3,2,1,0:T(8,128)(2,1)S(1)}, bf16[2,4,16,256]{3,2,1,0:T(8,128)(2,1)S(1)}, f32[27,256]{1,0:T(8,128)S(1)}) custom-call(bf16[2,4,16,256]{3,2,1,0:T(8,128)(2,1)} %q_hbm.1, bf16[2,4,16,256]{3,2,1,0:T(8,128)(2,1)} %k_hbm.1, bf16[2,4,16,256]{3,2,1,0:T(8,128)(2,1)} %v_hbm.1, ...), custom_call_target="tpu_custom_call" | custom-call | tf_op jit(solution)/shard_map/pallas_call | solution.py:732
  32.9 0.7 %shard_map.94 = (bf16[2,4,16,256]{3,2,1,0:T(8,128)(2,1)}, bf16[2,4,16,256]{3,2,1,0:T(8,128)(2,1)}, bf16[2,4,16,256]{3,2,1,0:T(8,128)(2,1)}, f32[27,256]{1,0:T(8,128)}) custom-call(bf16[2,4,16,256]{3,2,1,0:T(8,128)(2,1)S(1)} %get-tuple-element.8.refs_0_, bf16[2,4,16,256]{3,2,1,0:T(8,128)(2,1)S(1)} %get-tuple-element.9.refs_1_, ...), custom_call_target="tpu_custom_call" | custom-call | tf_op jit(solution)/shard_map/pallas_call | solution.py:778
